TPU v7x, 32 devices: a whole 2x2x4 slice. The times are simulated.
32 devices in a mesh: owner: 16 (over z, y, x), section: 2 (over core).
Axes of the slice: x: 2, y: 2, z: 4, core: 2. Of those that a mesh axis runs over, the one named last changes fastest.
Arguments:
- memory: bfloat16 [65536, 512], P('owner', 'section'), may hold values from -6 to 6
- last_seen: int32 [65536], P('owner'), may hold values from 0 to 4095
- ends_owner: int32 [2, 1024, 2], P(None, 'owner'), may hold values from 0 to 15, all different within a row; in each aligned block of 64 rows (0 to 63, 64 to 127, ..., all dimensions but the last counted through in order) at most 16 rows name the same one
- ends_row: int32 [2, 1024, 2], P(None, 'owner'), may hold values from 0 to 4095
- event_order: int32 [2, 1024], P(None, 'owner'), may hold values from 0 to 1023, each once within a row
- event_time: int32 [2, 1024], P(None, 'owner'), may hold values from 0 to 4095
- edge_feat: bfloat16 [2, 1024, 128], P(None, 'owner'), may hold values from -6 to 6
- nb_owner: int32 [2, 1024, 40, 1], P(None, 'owner'), may hold values from 0 to 15; in each aligned block of 2560 rows (0 to 2559, 2560 to 5119, ..., all dimensions but the last counted through in order) at most 240 rows name the same one
- nb_row: int32 [2, 1024, 40], P(None, 'owner'), may hold values from 0 to 4095
- nb_time: int32 [2, 1024, 40], P(None, 'owner'), may hold values from 0 to 4095
- time_freq: float32 [128], replicated, may hold values from 0.001 to 1
- time_phase: float32 [128], replicated, may hold values from -3.140625 to 3.140625
- gru_in: bfloat16 [1280, 3, 512], P(None, None, 'section'), may hold values from -0.15625 to 0.15625
- gru_hid: bfloat16 [512, 3, 512], P(None, None, 'section'), may hold values from -0.25 to 0.25
- gru_bias: float32 [2, 3, 512], P(None, None, 'section'), may hold values from -3 to 3
- query_w: bfloat16 [512, 512], replicated, may hold values from -0.25 to 0.25
- key_w: bfloat16 [512, 512], replicated, may hold values from -0.25 to 0.25
- value_w: bfloat16 [512, 512], replicated, may hold values from -0.25 to 0.25
- time_key: bfloat16 [128, 512], replicated, may hold values from -0.5 to 0.5
- time_value: bfloat16 [128, 512], replicated, may hold values from -0.5 to 0.5
- out_w: bfloat16 [512, 512], replicated, may hold values from -0.25 to 0.25
Outputs:
- updated_memory: bfloat16 [65536, 512], P('owner', 'section')
- embedding: bfloat16 [2, 1024, 2, 512], P(None, 'owner', None, 'section')
Inputs may be any that keep to these rules, and one draw needn't show every extreme that they name: `ends_owner`: in every batch the two endpoints of an event have different owners; of the events of one device (64 in a row in each batch), at most 16 name one owner, and in each draw some owner is named by exactly 16. `nb_owner`: in every batch, of the 2560 neighbor entries of one device's events, at most 240 name one owner, and in each draw some owner is named by exactly 240. `event_order`: each batch's row is a permutation of 0 to 1023; a larger value is a later event.
All inputs are finite; a program needn't handle non-finite values.
Results may differ from a plain program's by a relative error of at most 0.0029.
Values may be sent and summed in bfloat16 or wider, within the bound.
A program may use at most 128 MiB of HBM per device.

v0:
```python
import functools
import math

import jax
import jax.numpy as jnp
from jax import lax
from jax.experimental import pallas as pl
from jax.experimental.pallas import tpu as pltpu
from jax.sharding import PartitionSpec as P

HEADS = 2
BATCHES = 2
BF = jnp.bfloat16
F32 = jnp.float32


def time_code(delta, time_freq, time_phase):
    angle = delta.astype(F32)[..., None] * time_freq + time_phase
    return jnp.cos(angle).astype(BF)


def owner_hits(own, owners):
    return own[..., None] == jnp.arange(owners, dtype=jnp.int32)


def ranks(hits, block):
    batches, total, owners = hits.shape
    parts = total // block
    cut = hits.astype(BF).reshape(batches, parts, block, owners)
    below = jnp.tril(jnp.ones((block, block), BF), -1)
    within = jnp.einsum("ij,bkjo->bkio", below, cut, preferred_element_type=F32)
    sums = jnp.sum(cut.astype(F32), axis=2)
    before = jnp.cumsum(sums, axis=1) - sums
    count = within + before[:, :, None]
    picked = jnp.sum(jnp.where(hits.reshape(cut.shape), count, 0.0), axis=3)
    return picked.reshape(batches, total).astype(jnp.int32)


def table_of(hits, rank, size, values):
    place = (rank[..., None] == jnp.arange(size, dtype=jnp.int32)).astype(BF)

    def digit(part):
        lhs = jnp.where(hits, part[..., None].astype(F32), 0.0).astype(BF)
        return jnp.einsum("bno,bns->bos", lhs, place, preferred_element_type=F32)

    return (digit(values // 64) * 64.0 + digit(values % 64)).astype(jnp.int32)


def attend_kernel(scale, group, near, code, query, wide, twide, out, num, den):
    step = pl.program_id(0)
    points, head = query.shape

    @pl.when(step == 0)
    def _():
        num[...] = jnp.zeros_like(num)
        den[...] = jnp.zeros_like(den)

    both = jnp.dot(near[...], wide[...], preferred_element_type=F32) + jnp.dot(
        code[...], twide[...], preferred_element_type=F32
    )
    q = query[...]
    for j in range(group):
        rows = both[j * points : (j + 1) * points]
        score = jnp.sum(rows[:, :head] * q, axis=1, keepdims=True) * scale
        weight = jnp.exp(score)
        den[...] += jnp.broadcast_to(weight, den.shape)
        num[...] += weight * rows[:, head:]

    @pl.when(step == pl.num_programs(0) - 1)
    def _():
        out[...] = num[...] / den[:, :1]


def attend(near, code, query, wide, twide, neighbors, scale):
    points, head = query.shape
    group = next(g for g in (4, 2, 1) if neighbors % g == 0)
    rows = group * points
    return pl.pallas_call(
        functools.partial(attend_kernel, scale, group),
        out_shape=jax.ShapeDtypeStruct((points, head), F32),
        grid=(neighbors // group,),
        in_specs=[
            pl.BlockSpec((rows, near.shape[1]), lambda i: (i, 0)),
            pl.BlockSpec((rows, code.shape[1]), lambda i: (i, 0)),
            pl.BlockSpec(query.shape, lambda i: (0, 0)),
            pl.BlockSpec(wide.shape, lambda i: (0, 0)),
            pl.BlockSpec(twide.shape, lambda i: (0, 0)),
        ],
        out_specs=pl.BlockSpec((points, head), lambda i: (0, 0)),
        scratch_shapes=[pltpu.VMEM((points, head), F32), pltpu.VMEM((points, 128), F32)],
        compiler_params=pltpu.CompilerParams(vmem_limit_bytes=24 * 1024 * 1024),
        cost_estimate=pl.CostEstimate(
            flops=2 * near.shape[0] * (near.shape[1] + code.shape[1]) * wide.shape[1],
            bytes_accessed=2 * near.size + 2 * code.size + 2 * wide.size,
            transcendentals=near.shape[0],
        ),
    )(near, code, query, wide, twide)


def write_rows(memory, rows, order, values):
    count = memory.shape[0]
    beaten = jnp.any((rows[:, None] == rows[None, :]) & (order[None, :] > order[:, None]), axis=1)
    place = jnp.where((rows >= 0) & ~beaten, rows, count)
    return memory.at[place].set(values, mode="drop")


def on_device(
    memory,
    last_seen,
    ends_owner,
    ends_row,
    event_order,
    event_time,
    edge_feat,
    nb_owner,
    nb_row,
    nb_time,
    time_freq,
    time_phase,
    gru_in,
    gru_hid,
    gru_bias,
    query_w,
    key_w,
    value_w,
    time_key,
    time_value,
    out_w,
):
    owners = lax.axis_size("owner")
    sections = lax.axis_size("section")
    count, half = memory.shape
    width = half * sections
    events = ends_owner.shape[1]
    points = 2 * events
    neighbors = nb_row.shape[2] // 2
    head_dim = width // HEADS
    cap = max(4, 4 * events // owners)
    capn = max(8, 3 * neighbors * events // owners)
    slots = cap + capn
    total = owners * points
    scale = 1.0 / math.sqrt(head_dim)
    section_pos = lax.axis_index("section")
    owner_pos = lax.axis_index("owner")

    def by_neighbor(x):
        return x.reshape(BATCHES, points, neighbors).swapaxes(1, 2)

    end_own = ends_owner.reshape(BATCHES, points)
    end_row = ends_row.reshape(BATCHES, points)
    near_own = by_neighbor(nb_owner[..., 0]).reshape(BATCHES, -1)
    near_row = by_neighbor(nb_row).reshape(BATCHES, -1)
    order_two = jnp.repeat(event_order, 2, axis=1)
    time_two = jnp.repeat(event_time, 2, axis=1)
    end_hits = owner_hits(end_own, owners)
    near_hits = owner_hits(near_own, owners)
    end_rank = ranks(end_hits, points)
    near_rank = ranks(near_hits, points)
    local = jnp.broadcast_to(jnp.arange(points, dtype=jnp.int32), (BATCHES, points))
    asked = jnp.concatenate(
        [
            table_of(end_hits, end_rank, cap, end_row + 1),
            table_of(near_hits, near_rank, capn, near_row + 1),
            table_of(end_hits, end_rank, cap, order_two),
            table_of(end_hits, end_rank, cap, local),
        ],
        axis=2,
    )
    got = lax.all_to_all(asked.swapaxes(0, 1), "owner", split_axis=0, concat_axis=0, tiled=True)
    end_slot = end_own * slots + end_rank
    near_slot = near_own * slots + cap + near_rank

    end_id = end_own * count + end_row
    near_id = near_own * count + near_row
    mine = owner_pos * points + jnp.arange(points, dtype=jnp.int32)
    meta = jnp.stack([end_id[0], order_two[0] * total + mine, time_two[0]])
    all_meta = lax.all_gather(meta, "owner", axis=1, tiled=True)
    all_seen = lax.all_gather(last_seen, "owner", axis=0, tiled=True)
    base_seen = jnp.take(all_seen, end_id, mode="clip")

    came = []
    for batch in range(BATCHES):
        rows = jnp.maximum(got[:, batch, :slots] - 1, 0).reshape(-1)
        looked = jnp.take(memory, rows, axis=0, mode="clip").reshape(owners, slots, half)
        came.append(
            lax.all_to_all(looked, "owner", split_axis=0, concat_axis=0, tiled=True).reshape(-1, half)
        )

    start = section_pos * head_dim

    def columns(w, at, size):
        return lax.dynamic_slice_in_dim(w, at, size, 1)

    wide = jnp.concatenate([columns(key_w, start, head_dim), columns(value_w, start, head_dim)], axis=1)
    twide = jnp.concatenate(
        [columns(time_key, start, head_dim), columns(time_value, start, head_dim)], axis=1
    )
    query_cols = columns(query_w, start, head_dim)
    own_cols = columns(out_w, section_pos * half, half).astype(F32)
    gru_in_flat = gru_in.reshape(gru_in.shape[0], 3 * half)
    gru_hid_flat = gru_hid.reshape(width, 3 * half)
    near_code = time_code(time_two[:, None] - by_neighbor(nb_time), time_freq, time_phase)
    near_code = near_code.reshape(BATCHES, neighbors * points, -1)

    results = []
    updated = memory
    fresh_all = None
    for batch in range(BATCHES):
        table = came[batch]
        pick_end = end_slot[batch]
        pick_near = near_slot[batch]
        seen = base_seen[batch]
        if batch > 0:
            ids = jnp.concatenate([end_id[batch], near_id[batch]])
            best = jnp.max(
                jnp.where(all_meta[0][:, None] == ids[None, :], all_meta[1][:, None], -1), axis=0
            )
            written = best >= 0
            index = jnp.where(written, best % total, 0)
            table = jnp.concatenate([table, fresh_all], axis=0)
            newer = owners * slots + index
            pick_end = jnp.where(written[:points], newer[:points], pick_end)
            pick_near = jnp.where(written[points:], newer[points:], pick_near)
            since = jnp.take(all_meta[2], index[:points], mode="clip")
            seen = jnp.where(written[:points], since, seen)
        pick_other = pick_end.reshape(events, 2)[:, ::-1].reshape(points)
        picked = jnp.take(
            table, jnp.concatenate([pick_end, pick_other, pick_near]), axis=0, mode="clip"
        )
        full = lax.all_gather(picked, "section", axis=1, tiled=True)
        end_half = picked[:points].astype(F32)
        end_full = full[:points]
        other = full[points : 2 * points]
        near_full = full[2 * points :]
        self_code = time_code(time_two[batch] - seen, time_freq, time_phase)
        feat_two = jnp.repeat(edge_feat[batch], 2, axis=0)
        message = jnp.concatenate([end_full, other, self_code, feat_two], axis=1)
        from_msg = jnp.dot(message, gru_in_flat, preferred_element_type=F32)
        from_mem = jnp.dot(end_full, gru_hid_flat, preferred_element_type=F32)

        def block(x, i, side):
            return x[:, i * half : (i + 1) * half] + gru_bias[side, i]

        reset = jax.nn.sigmoid(block(from_msg, 0, 0) + block(from_mem, 0, 1))
        update = jax.nn.sigmoid(block(from_msg, 1, 0) + block(from_mem, 1, 1))
        cand = jnp.tanh(block(from_msg, 2, 0) + reset * block(from_mem, 2, 1))
        fresh = ((1.0 - update) * cand + update * end_half).astype(BF)
        fresh_all = lax.all_gather(fresh, "owner", axis=0, tiled=True)

        wrote = got[:, batch, :cap].reshape(-1) - 1
        order = got[:, batch, slots : slots + cap].reshape(-1)
        source = jnp.arange(owners, dtype=jnp.int32)[:, None] * points + got[:, batch, slots + cap :]
        values = jnp.take(fresh_all, source.reshape(-1), axis=0, mode="clip")
        updated = write_rows(updated, wrote, order, values)

        query = jnp.dot(end_full, query_cols, preferred_element_type=F32)
        attended = attend(near_full, near_code[batch], query, wide, twide, neighbors, scale)
        mixed = lax.all_gather(attended, "section", axis=1, tiled=True)
        emb = jnp.dot(mixed, own_cols, precision=lax.Precision.HIGHEST) + end_half
        results.append(emb.astype(BF).reshape(events, 2, half))
    return (updated, jnp.stack(results, axis=0))


def solution(mesh):
    in_specs = (
        P("owner", "section"),
        P("owner"),
        P(None, "owner", None),
        P(None, "owner", None),
        P(None, "owner"),
        P(None, "owner"),
        P(None, "owner", None),
        P(None, "owner", None, None),
        P(None, "owner", None),
        P(None, "owner", None),
        P(),
        P(),
        P(None, None, "section"),
        P(None, None, "section"),
        P(None, None, "section"),
        P(),
        P(),
        P(),
        P(),
        P(),
        P(),
    )
    out_specs = (P("owner", "section"), P(None, "owner", None, "section"))
    return jax.shard_map(
        on_device, mesh=mesh, in_specs=in_specs, out_specs=out_specs, check_vma=False
    )
```

profile of v0, /device:TPU:0, one launch (start us, length us, event | category | flops | bytes accessed | tf_op | source)
XLA Modules:
  0.0 372.7 jit_solution(8658875751913036181)
XLA Ops:
  7.2 1.6 copy.76
  9.2 0.2 convert_reduce_fusion
  9.4 0.3 fusion.6
  10.4 0.2 fusion.18
  11.3 0.2 reshape.601
  11.7 0.9 fusion
  12.5 0.9 fusion.11
  13.9 15.6 %all_to_all.15 = s32[16,2,288]{2,1,0:T(2,128)S(1)} all-to-all(s32[16,2,288]{2,1,0:T(2,128)S(1)} %copy.57), channel_id=1, replica_groups=mesh['owner'=16,'section'=2] {'owner'}, dimensions={0} | all-to-all | bytes 73728 | tf_op jit(solution)/shard_map/all_to_all | solution.py:169
  29.6 16.9 %gather_fusion = bf16[4096,256]{1,0:T(8,128)(2,1)} fusion(bf16[4096,256]{1,0:T(8,128)(2,1)S(1)} %copy.76, s32[4096]{0:T(1024)S(1)} %broadcast_clamp_fusion.1), kind=kCustom, calls=%fused_computation | custom fusion | bytes 4210688 | tf_op jit(solution)/shard_map/jit(_take)/gather | solution.py:184
  46.5 4.6 %all-to-all-start.1 = ((bf16[16,256,256]{2,1,0:T(8,128)(2,1)}), bf16[16,256,256]{2,1,0:T(8,128)(2,1)}, u32[]{:S(2)}, u32[]{:S(2)}) async-start(bf16[16,256,256]{2,1,0:T(8,128)(2,1)} %bitcast.109), calls=%async_computation.1 | async-start | bytes 4194304 | tf_op jit(solution)/shard_map/all_to_all | solution.py:186
  51.9 0.5 slice_bitcast_fusion.3
  52.8 65.6 %all_gather.27 = s32[3,2048]{1,0:T(4,128)S(1)} all-gather(s32[3,128]{1,0:T(4,128)S(1)} %pad_add_fusion.3), channel_id=1, replica_groups=mesh['owner'=16,'section'=2] {'owner'}, dimensions={1}, use_global_device_ids=true | all-gather | bytes 26112 | tf_op jit(solution)/shard_map/all_gather | solution.py:177
  118.4 0.6 slice_reduce_fusion
  119.2 9.3 %gather_fusion.1 = bf16[2816,256]{1,0:T(8,128)(2,1)} fusion(bf16[4096,256]{1,0:T(8,128)(2,1)} %bitcast.12, s32[3072]{0:T(1024)S(1)} %pad_clamp_fusion.1), kind=kCustom, calls=%fused_computation.1 | custom fusion | bytes 2894848 | tf_op jit(solution)/shard_map/jit(_take)/gather | solution.py:227
  128.5 4.0 %select_reduce_fusion = s32[2688]{0:T(1024)S(1)} fusion(s32[2048]{0:T(1024)S(1)} %bitcast.136, s32[2688]{0:T(1024)S(1)} %pad_add_fusion.1, s32[2048]{0:T(1024)S(1)} %bitcast.137), kind=kLoop, calls=%fused_computation.10 | loop fusion | flops 16512384 | bytes 37888 | tf_op jit(solution)/shard_map/reduce_max | solution.py:215
  132.5 43.4 %all_gather.25 = s32[65536]{0:T(1024)} all-gather(s32[4096]{0:T(1024)S(1)} %copy-done.11), channel_id=1, replica_groups=mesh['owner'=16,'section'=2] {'owner'}, dimensions={0}, use_global_device_ids=true | all-gather | bytes 278528 | tf_op jit(solution)/shard_map/all_gather | solution.py:178
  175.9 0.6 fusion.171
  176.5 17.0 %gather_fusion.3 = bf16[4096,256]{1,0:T(8,128)(2,1)} fusion(bf16[4096,256]{1,0:T(8,128)(2,1)S(1)} %copy.76, s32[4096]{0:T(1024)S(1)} %broadcast_clamp_fusion), kind=kCustom, calls=%fused_computation.4 | custom fusion | bytes 4210688 | tf_op jit(solution)/shard_map/jit(_take)/gather | solution.py:184
  193.5 3.7 all-to-all-start.2
  197.6 1.4 copy.60
  199.1 4.0 %copy.59 = bf16[1280,3,256]{0,2,1:T(8,128)(2,1)} copy(bf16[1280,3,256]{2,0,1:T(8,128)(2,1)} %param.33) | data formatting | bytes 3932160 | tf_op args[12]
  203.0 1.7 gather_fusion.5
  204.7 2.2 gather_fusion.2
  206.9 1.2 fusion.143
  208.1 1.8 cosine_convert_fusion.1
  209.9 1.0 fusion.168
  210.9 1.3 fusion.164
  212.3 2.3 fusion.20
  214.6 1.6 fusion.51
  216.3 0.2 all-gather.13.cloned.1.call-start
  216.5 1.5 reduce_max.12
  218.0 0.7 squeeze.60
  218.7 1.3 broadcast_compare_fusion
  220.0 1.2 fusion.166
  221.5 0.7 slice_select_fusion.1
  222.2 0.6 pad_add_fusion.2
  222.8 6.4 %all-to-all-done.2 = bf16[16,256,256]{2,1,0:T(8,128)(2,1)S(1)} async-done(((bf16[16,256,256]{2,1,0:T(8,128)(2,1)}), bf16[16,256,256]{2,1,0:T(8,128)(2,1)S(1)}, u32[]{:S(2)}, u32[]{:S(2)}) %all-to-all-start.2) | async-done | bytes 2097184 | tf_op jit(solution)/shard_map/all_to_all | solution.py:186
  229.2 44.1 %all-gather.7.cloned.1.call-done = bf16[2048,256]{1,0:T(8,128)(2,1)} async-done(((bf16[128,256]{1,0:T(8,128)(2,1)}), bf16[2048,256]{1,0:T(8,128)(2,1)}) %all-gather.7.cloned.1.call-update) | async-done | bytes 1048592 | tf_op jit(solution)/shard_map/all_gather | solution.py:248
  273.4 3.1 pad_maximum_fusion
  276.5 9.7 %gather_fusion.4 = bf16[2816,256]{1,0:T(8,128)(2,1)} fusion(bf16[6144,256]{1,0:T(8,128)(2,1)} %pad_maximum_fusion, s32[3072]{0:T(1024)S(1)} %pad_clamp_fusion), kind=kCustom, calls=%fused_computation.5 | custom fusion | bytes 2894848 | tf_op jit(solution)/shard_map/jit(_take)/gather | solution.py:227
  287.2 0.2 copy-done.3
  287.3 1.0 constant_dynamic-slice_fusion.2
  288.4 9.2 %cosine_convert_fusion = bf16[2,20,128,128]{3,2,1,0:T(8,128)(2,1)S(1)} fusion(f32[128]{0:T(128)S(1)} %copy-done.25, f32[128]{0:T(128)S(1)} %copy-done.26, f32[2,20,128]{2,1,0:T(8,128)S(1)} %copy.62), kind=kLoop, calls=%fused_computation.15 | loop fusion | flops 1966080 | bytes 1332224 | tf_op jit(solution)/shard_map/convert_element_type | solution.py:19
  297.7 0.2 slice_reduce_fusion.2
  298.4 0.2 and_reduce_fusion
  298.6 0.2 and_reduce_fusion.1
  298.9 1.0 fusion.167
  299.9 2.3 fusion.28
  302.3 1.3 fusion.161
  303.6 1.6 fusion.53
  305.4 1.9 slice.327.near
  307.4 1.1 fusion.41.query
  308.5 3.4 shard_map.212
  311.9 2.0 all_gather.30
  313.9 1.1 fusion.7
  315.1 6.7 %scatter_custom_fusion = bf16[4096,256]{1,0:T(8,128)(2,1)} fusion(bf16[4096,256]{1,0:T(8,128)(2,1)} %copy-done.1, s32[256]{0:T(256)S(1)} %bitcast.141, bf16[2048,256]{1,0:T(8,128)(2,1)} %all-gather.7.cloned.1.call-done, s32[1024]{0:T(1024)S(1)} %pad_clamp_fusion.4), kind=kCustom, calls=%fused_computation.135 | custom fusion | bytes 2097152 | tf_op jit(solution)/shard_map/scatter | solution.py:104
  321.7 1.9 slice.329.near
  323.6 1.1 fusion.39.query
  324.8 3.4 shard_map.213
  328.2 2.2 all_gather.31
  330.4 1.1 fusion.8
  331.5 0.8 pad_maximum_fusion.3
  332.4 27.1 %all-gather.9.cloned.1.call-done = bf16[2048,256]{1,0:T(8,128)(2,1)} async-done(((bf16[128,256]{1,0:T(8,128)(2,1)}), bf16[2048,256]{1,0:T(8,128)(2,1)}) %all-gather.9.cloned.1.call-update) | async-done | bytes 1048592 | tf_op jit(solution)/shard_map/all_gather | solution.py:248
  359.5 6.7 %scatter_custom_fusion.1 = bf16[4096,256]{1,0:T(8,128)(2,1)} fusion(bf16[4096,256]{1,0:T(8,128)(2,1)} %scatter_custom_fusion, s32[256]{0:T(256)S(1)} %bitcast.140, bf16[2048,256]{1,0:T(8,128)(2,1)} %all-gather.9.cloned.1.call-done, s32[1024]{0:T(1024)S(1)} %pad_clamp_fusion.2), kind=kCustom, calls=%fused_computation.133 | custom fusion | bytes 2097152 | tf_op jit(solution)/shard_map/scatter | solution.py:104
  (167 shorter events, 6.2 us)
Async XLA Ops:
  7.2 300.2 %copy-start = (bf16[512,512]{1,0:T(8,128)(2,1)S(1)}, bf16[512,512]{1,0:T(8,128)(2,1)}, u32[]{:S(2)}) copy-start(bf16[512,512]{1,0:T(8,128)(2,1)} %param.36) | copy-start | bytes 1572868
  7.2 2.9 copy-start.20
  7.2 3.5 copy-start.21
  7.2 1.7 copy-start.5
  7.2 2.5 copy-start.6
  8.9 167.7 %copy-start.1 = (bf16[4096,256]{1,0:T(8,128)(2,1)}, bf16[4096,256]{1,0:T(8,128)(2,1)S(1)}, u32[]{:S(2)}) copy-start(bf16[4096,256]{1,0:T(8,128)(2,1)S(1)} %copy.76) | copy-start | bytes 6291460
  8.9 2.4 copy-start.27
  46.5 4.9 %copy-start.23 = (s32[2,64]{1,0:T(2,128)S(1)}, s32[2,64]{1,0:T(2,128)}, u32[]{:S(2)}) copy-start(s32[2,64]{1,0:T(2,128)} %param.26) | copy-start | bytes 1540
  46.5 72.6 %all-to-all-start.1 = ((bf16[16,256,256]{2,1,0:T(8,128)(2,1)}), bf16[16,256,256]{2,1,0:T(8,128)(2,1)}, u32[]{:S(2)}, u32[]{:S(2)}) async-start(bf16[16,256,256]{2,1,0:T(8,128)(2,1)} %bitcast.109), calls=%async_computation.1 | async-start | bytes 4194304 | tf_op jit(solution)/shard_map/all_to_all | solution.py:186
  51.1 158.8 %all-gather.11.cloned.1.call-start = ((), (), s32[]{:S(2)}) async-start(), calls=%async_computation.5 | async-start | bytes 4325376 | tf_op jit(solution)/shard_map/all_gather | solution.py:230
  119.1 13.4 %copy-start.11 = (s32[4096]{0:T(1024)S(1)}, s32[4096]{0:T(1024)}, u32[]{:S(2)}) copy-start(s32[4096]{0:T(1024)} %param.22) | copy-start | bytes 49156
  119.1 56.8 %copy-start.22 = (f32[2,3,256]{2,0,1:T(2,128)S(1)}, f32[2,3,256]{2,0,1:T(2,128)}, u32[]{:S(2)}) copy-start(f32[2,3,256]{2,0,1:T(2,128)} %param.35) | copy-start | bytes 18436
  132.5 74.4 %copy-start.4 = (s32[2688]{0:T(1024)}, s32[2688]{0:T(1024)S(1)}, u32[]{:S(2)}) copy-start(s32[2688]{0:T(1024)S(1)} %get-tuple-element.37) | copy-start | bytes 32260
  176.5 38.1 %copy-start.12 = (f32[1,1,256]{2,0,1:T(1,128)}, f32[1,1,256]{2,0,1:T(1,128)S(1)}, u32[]{:S(2)}) copy-start(f32[1,1,256]{2,0,1:T(1,128)S(1)} %get-tuple-element.40) | copy-start | bytes 3076
  193.5 35.7 %all-to-all-start.2 = ((bf16[16,256,256]{2,1,0:T(8,128)(2,1)}), bf16[16,256,256]{2,1,0:T(8,128)(2,1)S(1)}, u32[]{:S(2)}, u32[]{:S(2)}) async-start(bf16[16,256,256]{2,1,0:T(8,128)(2,1)} %bitcast.108), calls=%async_computation.2 | async-start | bytes 4194304 | tf_op jit(solution)/shard_map/all_to_all | solution.py:186
  197.2 76.2 %all-gather.7.cloned.1.call-start = ((), (), s32[]{:S(2)}) async-start(), calls=%async_computation.3 | async-start | bytes 1114112 | tf_op jit(solution)/shard_map/all_gather | solution.py:248
  199.1 9.1 %copy-start.8 = (bf16[2,64,128]{2,1,0:T(8,128)(2,1)S(1)}, bf16[2,64,128]{2,1,0:T(8,128)(2,1)}, u32[]{:S(2)}) copy-start(bf16[2,64,128]{2,1,0:T(8,128)(2,1)} %param.27) | copy-start | bytes 98308
  210.9 3.7 copy-start.14
  210.9 3.7 copy-start.16
  210.9 3.7 copy-start.18
  216.3 82.6 %all-gather.13.cloned.1.call-start = ((), (), s32[]{:S(2)}) async-start(), calls=%async_computation.6 | async-start | bytes 4325376 | tf_op jit(solution)/shard_map/all_gather | solution.py:230
  276.5 10.0 %copy-start.7 = (s32[2,64,40]{1,2,0:T(8,128)S(1)}, s32[2,64,40]{1,2,0:T(8,128)}, u32[]{:S(2)}) copy-start(s32[2,64,40]{1,2,0:T(8,128)} %param.30) | copy-start | bytes 61444
  276.5 10.2 %copy-start.24 = (s32[2,64]{1,0:T(2,128)S(1)}, s32[2,64]{1,0:T(2,128)}, u32[]{:S(2)}) copy-start(s32[2,64]{1,0:T(2,128)} %param.26) | copy-start | bytes 1540
  286.2 0.9 copy-start.9
  286.2 1.0 copy-start.10
  286.2 1.2 copy-start.3
  286.2 2.2 copy-start.25
  286.2 2.2 copy-start.26
  286.2 73.3 %all-gather.9.cloned.1.call-start = ((), (), s32[]{:S(2)}) async-start(), calls=%async_computation.4 | async-start | bytes 1114112 | tf_op jit(solution)/shard_map/all_gather | solution.py:248
  299.9 3.7 copy-start.13
  299.9 3.7 copy-start.15
  299.9 3.7 copy-start.17
  299.9 3.7 copy-start.19
  308.5 5.4 %copy-start.2 = (bf16[512,512]{1,0:T(8,128)(2,1)S(1)}, bf16[512,512]{1,0:T(8,128)(2,1)}, u32[]{:S(2)}) copy-start(bf16[512,512]{1,0:T(8,128)(2,1)} %param.41) | copy-start | bytes 1572868
Sparse Core Ops, SparseCore 0:
  128.6 13.8 all-gather.10
  216.4 56.9 all-gather.6
  286.3 10.1 all-gather.12
  305.3 54.0 all-gather.8
where the time goes:
time: 374 us; the launch traced here: 373 us
  blocking collectives  129 us (34%)
  local copies, waits for them, and re-layouts  92.6 us (25%)
  waiting for transfers between devices  77.7 us (21%)
  other arithmetic  28.8 us (8%)
  matrix products  14.7 us (4%)
  between operations  14.7 us (4%)
  starting transfers between devices  8.63 us (2%)
  Pallas kernels  6.79 us (2%)
    all_gather x2, waiting for transfers between devices, on_device(): fresh_all = lax.all_gather(fresh, 'owner', axis=0, tiled=True)  71.2 us
    all_gather x1, blocking collectives, on_device(): all_meta = lax.all_gather(meta, 'owner', axis=1, tiled=True)  65.6 us
    all_gather x1, blocking collectives, on_device(): all_seen = lax.all_gather(last_seen, 'owner', axis=0, tiled=True)  43.4 us
    gather x2, local copies, waits for them, and re-layouts, on_device(): jnp.take(memory, rows, axis=0, mode='clip').reshape(owners, slots, half)  33.9 us
    gather x2, local copies, waits for them, and re-layouts, on_device(): jnp.take(table, jnp.concatenate([pick_end, pick_other, pick_near]), axis=...  19 us
    all_to_all x1, blocking collectives, on_device(): lax.all_to_all(asked.swapaxes(0, 1), 'owner', split_axis=0, concat_axis=0...  15.6 us
    scatter x2, local copies, waits for them, and re-layouts, write_rows(): return memory.at[place].set(values, mode='drop')  13.4 us
    convert_element_type x2, other arithmetic, time_code(): return jnp.cos(angle).astype(BF)  11 us
  transfers between devices with their start and end apart: 6, of which 3 were waited for; matrix products, arithmetic and copies ran while one was open for 21% of the time, Pallas kernels for 2%

commit v1 on v0

--- a/solution.py
+++ b/solution.py
@@ -29,8 +29,9 @@
     cut = hits.astype(BF).reshape(batches, parts, block, owners)
     below = jnp.tril(jnp.ones((block, block), BF), -1)
     within = jnp.einsum("ij,bkjo->bkio", below, cut, preferred_element_type=F32)
-    sums = jnp.sum(cut.astype(F32), axis=2)
-    before = jnp.cumsum(sums, axis=1) - sums
+    sums = jnp.sum(cut.astype(F32), axis=2).astype(BF)
+    earlier = jnp.tril(jnp.ones((parts, parts), BF), -1)
+    before = jnp.einsum("kl,blo->bko", earlier, sums, preferred_element_type=F32)
     count = within + before[:, :, None]
     picked = jnp.sum(jnp.where(hits.reshape(cut.shape), count, 0.0), axis=3)
     return picked.reshape(batches, total).astype(jnp.int32)
@@ -90,11 +91,15 @@
         scratch_shapes=[pltpu.VMEM((points, head), F32), pltpu.VMEM((points, 128), F32)],
         compiler_params=pltpu.CompilerParams(vmem_limit_bytes=24 * 1024 * 1024),
         cost_estimate=pl.CostEstimate(
-            flops=2 * near.shape[0] * (near.shape[1] + code.shape[1]) * wide.shape[1],
-            bytes_accessed=2 * near.size + 2 * code.size + 2 * wide.size,
-            transcendentals=near.shape[0],
+            flops=2 * code.shape[0] * (near.shape[1] + code.shape[1]) * wide.shape[1],
+            bytes_accessed=2 * code.shape[0] * near.shape[1] + 2 * code.size + 2 * wide.size,
+            transcendentals=code.shape[0],
         ),
     )(near, code, query, wide, twide)
+
+
+def exchange(x):
+    return lax.all_to_all(x, "owner", split_axis=0, concat_axis=0, tiled=True)
 
 
 def write_rows(memory, rows, order, values):
@@ -166,25 +171,34 @@
         ],
         axis=2,
     )
-    got = lax.all_to_all(asked.swapaxes(0, 1), "owner", split_axis=0, concat_axis=0, tiled=True)
-    end_slot = end_own * slots + end_rank
-    near_slot = near_own * slots + cap + near_rank
-
     end_id = end_own * count + end_row
     near_id = near_own * count + near_row
     mine = owner_pos * points + jnp.arange(points, dtype=jnp.int32)
-    meta = jnp.stack([end_id[0], order_two[0] * total + mine, time_two[0]])
-    all_meta = lax.all_gather(meta, "owner", axis=1, tiled=True)
-    all_seen = lax.all_gather(last_seen, "owner", axis=0, tiled=True)
-    base_seen = jnp.take(all_seen, end_id, mode="clip")
-
-    came = []
-    for batch in range(BATCHES):
+    meta = jnp.concatenate([end_id[0], order_two[0] * total + mine, time_two[0]])
+    per_batch = slots + 2 * cap
+    asked = jnp.concatenate(
+        [
+            asked.swapaxes(0, 1).reshape(owners, BATCHES * per_batch),
+            jnp.broadcast_to(meta, (owners, 3 * points)),
+        ],
+        axis=1,
+    )
+    answer = exchange(asked)
+    got = answer[:, : BATCHES * per_batch].reshape(owners, BATCHES, per_batch)
+    all_meta = answer[:, BATCHES * per_batch :].reshape(owners, 3, points)
+    all_meta = [all_meta[:, i].reshape(total) for i in range(3)]
+    end_pos = end_own * cap + end_rank
+    end_slot = end_own * slots + end_rank
+    near_slot = near_own * slots + cap + near_rank
+
+    asked_ends = jnp.maximum(got[:, :, :cap] - 1, 0).reshape(-1)
+    stamps = jnp.take(last_seen, asked_ends, mode="clip").reshape(owners, BATCHES * cap)
+    stamps = exchange(stamps).reshape(owners, BATCHES, cap).swapaxes(0, 1).reshape(BATCHES, -1)
+    base_seen = jnp.stack([jnp.take(stamps[b], end_pos[b], mode="clip") for b in range(BATCHES)])
+
+    def look(batch):
         rows = jnp.maximum(got[:, batch, :slots] - 1, 0).reshape(-1)
-        looked = jnp.take(memory, rows, axis=0, mode="clip").reshape(owners, slots, half)
-        came.append(
-            lax.all_to_all(looked, "owner", split_axis=0, concat_axis=0, tiled=True).reshape(-1, half)
-        )
+        return jnp.take(memory, rows, axis=0, mode="clip").reshape(owners, slots, half)
 
     start = section_pos * head_dim
 
@@ -201,6 +215,12 @@
     gru_hid_flat = gru_hid.reshape(width, 3 * half)
     near_code = time_code(time_two[:, None] - by_neighbor(nb_time), time_freq, time_phase)
     near_code = near_code.reshape(BATCHES, neighbors * points, -1)
+
+    first, second = exchange(look(0)), look(1)
+    first, second, near_code, gru_in_flat, gru_hid_flat = lax.optimization_barrier(
+        (first, second, near_code, gru_in_flat, gru_hid_flat)
+    )
+    came = [first.reshape(-1, half), exchange(second).reshape(-1, half)]
 
     results = []
     updated = memory
@@ -217,6 +237,7 @@
             )
             written = best >= 0
             index = jnp.where(written, best % total, 0)
+            table, results[0] = lax.optimization_barrier((table, results[0]))
             table = jnp.concatenate([table, fresh_all], axis=0)
             newer = owners * slots + index
             pick_end = jnp.where(written[:points], newer[:points], pick_end)
@@ -225,13 +246,13 @@
             seen = jnp.where(written[:points], since, seen)
         pick_other = pick_end.reshape(events, 2)[:, ::-1].reshape(points)
         picked = jnp.take(
-            table, jnp.concatenate([pick_end, pick_other, pick_near]), axis=0, mode="clip"
+            table, jnp.concatenate([pick_near, pick_end, pick_other]), axis=0, mode="clip"
         )
         full = lax.all_gather(picked, "section", axis=1, tiled=True)
-        end_half = picked[:points].astype(F32)
-        end_full = full[:points]
-        other = full[points : 2 * points]
-        near_full = full[2 * points :]
+        near_count = neighbors * points
+        end_half = picked[near_count : near_count + points].astype(F32)
+        end_full = full[near_count : near_count + points]
+        other = full[near_count + points :]
         self_code = time_code(time_two[batch] - seen, time_freq, time_phase)
         feat_two = jnp.repeat(edge_feat[batch], 2, axis=0)
         message = jnp.concatenate([end_full, other, self_code, feat_two], axis=1)
@@ -245,16 +266,21 @@
         update = jax.nn.sigmoid(block(from_msg, 1, 0) + block(from_mem, 1, 1))
         cand = jnp.tanh(block(from_msg, 2, 0) + reset * block(from_mem, 2, 1))
         fresh = ((1.0 - update) * cand + update * end_half).astype(BF)
-        fresh_all = lax.all_gather(fresh, "owner", axis=0, tiled=True)
-
         wrote = got[:, batch, :cap].reshape(-1) - 1
         order = got[:, batch, slots : slots + cap].reshape(-1)
-        source = jnp.arange(owners, dtype=jnp.int32)[:, None] * points + got[:, batch, slots + cap :]
-        values = jnp.take(fresh_all, source.reshape(-1), axis=0, mode="clip")
+        if batch + 1 < BATCHES:
+            fresh_all = exchange(jnp.broadcast_to(fresh, (owners, points, half))).reshape(total, half)
+            source = jnp.arange(owners, dtype=jnp.int32)[:, None] * points
+            source = source + got[:, batch, slots + cap :]
+            values = jnp.take(fresh_all, source.reshape(-1), axis=0, mode="clip")
+        else:
+            place = jnp.arange(owners * cap, dtype=jnp.int32)[:, None] == end_pos[batch][None, :]
+            sent = jnp.dot(place.astype(BF), fresh, preferred_element_type=F32).astype(BF)
+            values = exchange(sent.reshape(owners, cap, half)).reshape(-1, half)
         updated = write_rows(updated, wrote, order, values)
 
         query = jnp.dot(end_full, query_cols, preferred_element_type=F32)
-        attended = attend(near_full, near_code[batch], query, wide, twide, neighbors, scale)
+        attended = attend(full, near_code[batch], query, wide, twide, neighbors, scale)
         mixed = lax.all_gather(attended, "section", axis=1, tiled=True)
         emb = jnp.dot(mixed, own_cols, precision=lax.Precision.HIGHEST) + end_half
         results.append(emb.astype(BF).reshape(events, 2, half))

time: 374 us -> 280 us (0.75)
  blocking collectives: 129 us -> 20 us
  starting transfers between devices: 8.63 us -> 37.8 us
  waiting for transfers between devices: 77.7 us -> 56 us
  local copies, waits for them, and re-layouts: 92.6 us -> 96.4 us
    all_gather x2 -> x0, blocking collectives: 109 us -> none  [the longest x1 65.6 us: on_device(): all_meta = lax.all_gather(meta, 'owner', axis=1, tiled=True)]
    all_gather x2 -> x0, waiting for transfers between devices: 71.2 us -> none  [on_device(): fresh_all = lax.all_gather(fresh, 'owner', axis=0, tiled=True)]
    all_to_all x2 -> x5, waiting for transfers between devices: 6.4 us -> 52.5 us  [exchange(): return lax.all_to_all(x, 'owner', split_axis=0, concat_axis=0, tiled=True)]
    all_to_all x2 -> x5, starting transfers between devices: 8.28 us -> 37.7 us  [exchange(): return lax.all_to_all(x, 'owner', split_axis=0, concat_axis=0, tiled=True)]
    slice x6 -> x7, local copies, waits for them, and re-layouts: 6.5 us -> 1.17 us  [the longest x2 1 us: on_device(): end_full = full[near_count:near_count + points]]
    unnamed x64 -> x114, local copies, waits for them, and re-layouts: 7.87 us -> 12.4 us
    gather x5 -> x7, local copies, waits for them, and re-layouts: 55 us -> 59 us  [the longest x2 34 us: look(): jnp.take(memory, rows, axis=0, mode='clip').reshape(owners, slots, half)]
    scatter x2, local copies, waits for them, and re-layouts: 13.4 us -> 9.49 us  [write_rows(): return memory.at[place].set(values, mode='drop')]
  transfers between devices with their start and end apart: 6 -> 7, of which waited for: 3 -> 5; matrix products, arithmetic and copies ran while one was open for 21% -> 33% of each run, Pallas kernels for 2% -> 1%
where the time goes in v1:
time: 280 us; the launch traced here: 278 us
  local copies, waits for them, and re-layouts  96.4 us (34%)
  waiting for transfers between devices  56 us (20%)
  starting transfers between devices  37.8 us (13%)
  other arithmetic  31.2 us (11%)
  blocking collectives  20 us (7%)
  between operations  15.3 us (5%)
  matrix products  15 us (5%)
  Pallas kernels  6.76 us (2%)
    all_to_all x5, waiting for transfers between devices, exchange(): return lax.all_to_all(x, 'owner', split_axis=0, concat_axis=0, tiled=True)  52.5 us
    all_to_all x5, starting transfers between devices, exchange(): return lax.all_to_all(x, 'owner', split_axis=0, concat_axis=0, tiled=True)  37.7 us
    gather x2, local copies, waits for them, and re-layouts, look(): jnp.take(memory, rows, axis=0, mode='clip').reshape(owners, slots, half)  34 us
    gather x2, local copies, waits for them, and re-layouts, on_device(): jnp.take(table, jnp.concatenate([pick_near, pick_end, pick_other]), axis=...  19 us
    all_to_all x1, blocking collectives, exchange(): return lax.all_to_all(x, 'owner', split_axis=0, concat_axis=0, tiled=True)  15.6 us
    unnamed x114, local copies, waits for them, and re-layouts  12.4 us
    convert_element_type x2, other arithmetic, time_code(): return jnp.cos(angle).astype(BF)  11.6 us
    scatter x2, local copies, waits for them, and re-layouts, write_rows(): return memory.at[place].set(values, mode='drop')  9.49 us
  transfers between devices with their start and end apart: 7, of which 5 were waited for; matrix products, arithmetic and copies ran while one was open for 33% of the time, Pallas kernels for 1%

profile of v1, /device:TPU:0, one launch (start us, length us, event | category | flops | bytes accessed | tf_op | source)
XLA Modules:
  0.0 278.3 jit_solution(8918927522243490726)
XLA Ops:
  7.2 1.7 copy.87
  12.4 0.9 fusion
  13.3 0.9 fusion.11
  15.0 15.6 %all_to_all.41 = s32[16,1,960]{2,1,0:T(1,128)S(1)} all-to-all(s32[16,1,960]{2,1,0:T(1,128)S(1)} %copy.62), channel_id=1, replica_groups=mesh['owner'=16,'section'=2] {'owner'}, dimensions={0} | all-to-all | bytes 122880 | tf_op jit(solution)/shard_map/all_to_all | solution.py:102
  30.8 0.6 fusion.101
  31.4 17.0 %gather_fusion = bf16[4096,256]{1,0:T(8,128)(2,1)} fusion(bf16[4096,256]{1,0:T(8,128)(2,1)S(1)} %copy.87, s32[4096]{0:T(1024)S(1)} %broadcast_clamp_fusion.1), kind=kCustom, calls=%fused_computation | custom fusion | bytes 4210688 | tf_op jit(solution)/shard_map/jit(_take)/gather | solution.py:201
  48.4 4.4 %all-to-all-start.1 = ((bf16[16,256,256]{2,1,0:T(8,128)(2,1)}), bf16[16,256,256]{2,1,0:T(8,128)(2,1)}, u32[]{:S(2)}, u32[]{:S(2)}) async-start(bf16[16,256,256]{2,1,0:T(8,128)(2,1)} %bitcast.130), calls=%async_computation.1 | async-start | bytes 4194304 | tf_op jit(solution)/shard_map/all_to_all | solution.py:102
  53.1 0.7 broadcast_in_dim.245
  53.9 4.0 %copy.65 = bf16[1280,3,256]{0,2,1:T(8,128)(2,1)} copy(bf16[1280,3,256]{2,0,1:T(8,128)(2,1)} %param.33) | data formatting | bytes 3932160 | tf_op args[12]
  58.5 2.3 copy.66
  62.4 0.6 slice_reduce_fusion
  63.0 0.6 pad_clamp_fusion.1
  64.3 1.1 constant_dynamic-slice_fusion.2
  65.4 0.6 fusion.182
  66.1 0.7 slice_bitcast_fusion.2
  66.8 10.7 %cosine_convert_fusion = bf16[2,2560,128]{2,1,0:T(8,128)(2,1)} fusion(f32[128]{0:T(128)S(1)} %copy-done.40, f32[128]{0:T(128)} %param.31, f32[2,2560]{1,0:T(2,128)S(1)} %bitcast.145), kind=kLoop, calls=%fused_computation.16 | loop fusion | flops 1966080 | bytes 1332224 | tf_op jit(solution)/shard_map/convert_element_type | solution.py:19
  77.7 3.1 %gather_fusion.3 = s32[512]{0:T(512)S(1)} fusion(s32[4096]{0:T(1024)S(1)} %copy-done.6, s32[1024]{0:T(1024)S(1)} %pad_clamp_fusion.6), kind=kCustom, calls=%fused_computation.3 | custom fusion | bytes 6144 | tf_op jit(solution)/shard_map/jit(_take)/gather | solution.py:195
  80.9 0.7 all_to_all.30
  81.6 13.6 %all-to-all-done.1 = bf16[16,256,256]{2,1,0:T(8,128)(2,1)} async-done(((bf16[16,256,256]{2,1,0:T(8,128)(2,1)}), bf16[16,256,256]{2,1,0:T(8,128)(2,1)}, u32[]{:S(2)}, u32[]{:S(2)}) %all-to-all-start.1) | async-done | bytes 2097184 | tf_op jit(solution)/shard_map/all_to_all | solution.py:102
  95.2 9.7 %all-to-all-start.2 = ((s32[16,1,32]{2,1,0:T(1,128)}), s32[16,1,32]{2,1,0:T(1,128)S(1)}, u32[]{:S(2)}, u32[]{:S(2)}) async-start(s32[16,1,32]{2,1,0:T(1,128)} %all_to_all.30), calls=%async_computation.2 | async-start | bytes 16384 | tf_op jit(solution)/shard_map/all_to_all | solution.py:102
  105.0 17.0 %gather_fusion.1 = bf16[4096,256]{1,0:T(8,128)(2,1)} fusion(bf16[4096,256]{1,0:T(8,128)(2,1)S(1)} %copy.87, s32[4096]{0:T(1024)S(1)} %broadcast_clamp_fusion), kind=kCustom, calls=%fused_computation.1 | custom fusion | bytes 4210688 | tf_op jit(solution)/shard_map/jit(_take)/gather | solution.py:201
  122.0 9.3 %gather_fusion.2 = bf16[2816,256]{1,0:T(8,128)(2,1)} fusion(bf16[4096,256]{1,0:T(8,128)(2,1)} %bitcast.23, s32[3072]{0:T(1024)S(1)} %copy-done.14), kind=kCustom, calls=%fused_computation.2 | custom fusion | bytes 2894848 | tf_op jit(solution)/shard_map/jit(_take)/gather | solution.py:248
  131.9 7.0 %all-to-all-start.4 = ((bf16[16,256,256]{2,1,0:T(8,128)(2,1)}), bf16[16,256,256]{2,1,0:T(8,128)(2,1)}, u32[]{:S(2)}, u32[]{:S(2)}) async-start(bf16[16,256,256]{2,1,0:T(8,128)(2,1)} %bitcast.19), calls=%async_computation.4 | async-start | bytes 4194304 | tf_op jit(solution)/shard_map/all_to_all | solution.py:102
  138.9 4.0 %select_reduce_fusion = s32[2688]{0:T(1024)S(1)} fusion(s32[2048]{0:T(1024)S(1)} %bitcast.153, s32[2688]{0:T(1024)S(1)} %copy-done.23, s32[2048]{0:T(1024)S(1)} %bitcast.154), kind=kLoop, calls=%fused_computation.11 | loop fusion | flops 16512384 | bytes 37888 | tf_op jit(solution)/shard_map/reduce_max | solution.py:235
  142.9 0.6 reduce_max.12
  143.6 1.1 gather_fusion.6
  144.8 0.9 broadcast_compare_fusion
  145.8 1.0 fusion.178
  147.2 0.7 reduce.53
  148.2 1.4 gather_fusion.7
  149.6 1.4 gather_fusion.4
  151.6 0.9 cosine_convert_fusion.1
  152.6 1.0 fusion.180
  153.6 1.3 fusion.176
  154.9 2.3 fusion.20
  157.3 1.0 fusion.52
  158.3 22.6 %all-to-all-done.4 = bf16[16,256,256]{2,1,0:T(8,128)(2,1)} async-done(((bf16[16,256,256]{2,1,0:T(8,128)(2,1)}), bf16[16,256,256]{2,1,0:T(8,128)(2,1)}, u32[]{:S(2)}, u32[]{:S(2)}) %all-to-all-start.4) | async-done | bytes 2097184 | tf_op jit(solution)/shard_map/all_to_all | solution.py:102
  180.9 1.1 broadcast_in_dim.239
  182.0 9.8 %all-to-all-start.3 = ((bf16[16,128,256]{2,1,0:T(8,128)(2,1)}), bf16[16,128,256]{2,1,0:T(8,128)(2,1)}, u32[]{:S(2)}, u32[]{:S(2)}) async-start(bf16[16,128,256]{2,1,0:T(8,128)(2,1)} %broadcast_in_dim.239), calls=%async_computation.3 | async-start | bytes 2097152 | tf_op jit(solution)/shard_map/all_to_all | solution.py:102
  191.8 0.8 fusion.95
  192.9 1.5 slice_bitcast_fusion
  194.5 1.1 fusion.41.query
  195.6 3.4 %shard_map.212 = f32[128,256]{1,0:T(8,128)S(1)} custom-call(bf16[2816,512]{1,0:T(8,128)(2,1)S(1)} %copy-done.1, bf16[2560,128]{1,0:T(8,128)(2,1)S(1)} %get-tuple-element.37.code, f32[128,256]{1,0:T(8,128)S(1)} %fusion.41.query, bf16[512,512]{1,0:T(8,128)(2,1)S(1)} %pad_maximum_fusion.1.wide, bf16[128,512]{1,0:T(8,128)(2,1)S(1)} %pad_maximum_fusion.2.twide), custom_call_target="tpu_custom_call" | custom-call | flops 1677721600 | bytes 3801088 | tf_op jit(solution)/shard_map/pallas_call | solution.py:79
  199.0 2.0 all_gather.13
  201.0 1.1 fusion.7
  202.1 0.6 reshape.569
  202.8 12.7 %all-to-all-done.3 = bf16[16,128,256]{2,1,0:T(8,128)(2,1)} async-done(((bf16[16,128,256]{2,1,0:T(8,128)(2,1)}), bf16[16,128,256]{2,1,0:T(8,128)(2,1)}, u32[]{:S(2)}, u32[]{:S(2)}) %all-to-all-start.3) | async-done | bytes 1048608 | tf_op jit(solution)/shard_map/all_to_all | solution.py:102
  215.5 3.9 %pad_maximum_fusion = bf16[6144,256]{1,0:T(8,128)(2,1)} fusion(bf16[2048,256]{1,0:T(8,128)(2,1)} %bitcast.35, bf16[4096,256]{1,0:T(8,128)(2,1)} %bitcast.39), kind=kLoop, calls=%fused_computation.15 | loop fusion | flops 6291456 | bytes 6291456 | tf_op jit(solution)/shard_map/concatenate | solution.py:241
  219.3 9.7 %gather_fusion.5 = bf16[2816,256]{1,0:T(8,128)(2,1)} fusion(bf16[6144,256]{1,0:T(8,128)(2,1)} %pad_maximum_fusion, s32[3072]{0:T(1024)S(1)} %pad_clamp_fusion), kind=kCustom, calls=%fused_computation.6 | custom fusion | bytes 2894848 | tf_op jit(solution)/shard_map/jit(_take)/gather | solution.py:248
  230.5 6.8 %scatter_custom_fusion = bf16[4096,256]{1,0:T(8,128)(2,1)} fusion(bf16[4096,256]{1,0:T(8,128)(2,1)} %copy-done.3, s32[256]{0:T(256)S(1)} %bitcast.169, bf16[2048,256]{1,0:T(8,128)(2,1)} %bitcast.35, s32[1024]{0:T(1024)S(1)} %pad_clamp_fusion.4), kind=kCustom, calls=%fused_computation.138 | custom fusion | bytes 2097152 | tf_op jit(solution)/shard_map/scatter | solution.py:109
  237.3 3.5 %all-gather.7.cloned.1.call-done.near = bf16[2816,512]{1,0:T(8,128)(2,1)} async-done(((bf16[2816,256]{1,0:T(8,128)(2,1)}), bf16[2816,512]{1,0:T(8,128)(2,1)}) %all-gather.7.cloned.1.call-update) | async-done | bytes 2883600 | tf_op jit(solution)/shard_map/all_gather | solution.py:251
  240.7 1.1 fusion.39.query
  241.9 1.8 copy-done.2
  243.7 3.4 %shard_map.213 = f32[128,256]{1,0:T(8,128)S(1)} custom-call(bf16[2816,512]{1,0:T(8,128)(2,1)S(1)} %copy-done.2, bf16[2560,128]{1,0:T(8,128)(2,1)S(1)} %get-tuple-element.36.code, f32[128,256]{1,0:T(8,128)S(1)} %fusion.39.query, bf16[512,512]{1,0:T(8,128)(2,1)S(1)} %pad_maximum_fusion.1.wide, bf16[128,512]{1,0:T(8,128)(2,1)S(1)} %pad_maximum_fusion.2.twide), custom_call_target="tpu_custom_call" | custom-call | flops 1677721600 | bytes 3801088 | tf_op jit(solution)/shard_map/pallas_call | solution.py:79
  247.0 2.3 all_gather.15
  249.5 0.8 fusion.28
  250.8 1.9 convolution_convert_fusion
  252.7 6.8 %all-to-all-start.5 = ((bf16[16,16,256]{2,1,0:T(8,128)(2,1)}), bf16[16,16,256]{2,1,0:T(8,128)(2,1)S(1)}, u32[]{:S(2)}, u32[]{:S(2)}) async-start(bf16[16,16,256]{2,1,0:T(8,128)(2,1)} %bitcast.142), calls=%async_computation.5 | async-start | bytes 262144 | tf_op jit(solution)/shard_map/all_to_all | solution.py:102
  259.6 1.8 fusion.8
  261.3 0.9 stack_reshape.3
  262.2 1.7 pad_maximum_fusion.3
  263.9 3.5 %all-to-all-done.5 = bf16[16,16,256]{2,1,0:T(8,128)(2,1)S(1)} async-done(((bf16[16,16,256]{2,1,0:T(8,128)(2,1)}), bf16[16,16,256]{2,1,0:T(8,128)(2,1)S(1)}, u32[]{:S(2)}, u32[]{:S(2)}) %all-to-all-start.5) | async-done | bytes 131104 | tf_op jit(solution)/shard_map/all_to_all | solution.py:102
  267.4 2.7 scatter_fusion
  270.1 1.3 copy-done.5
  (232 shorter events, 11.9 us)
Async XLA Ops:
  7.2 187.3 %copy-start = (bf16[512,512]{1,0:T(8,128)(2,1)S(1)}, bf16[512,512]{1,0:T(8,128)(2,1)}, u32[]{:S(2)}) copy-start(bf16[512,512]{1,0:T(8,128)(2,1)} %param.36) | copy-start | bytes 1572868
  7.2 1.8 copy-start.46
  7.2 2.1 copy-start.47
  7.2 2.4 copy-start.51
  7.2 3.3 %copy-start.15 = (s32[2,64,40,1]{1,3,2,0:T(1,128)S(1)}, s32[2,64,40,1]{1,3,2,0:T(1,128)}, u32[]{:S(2)}) copy-start(s32[2,64,40,1]{1,3,2,0:T(1,128)} %param.28) | copy-start | bytes 61444
  7.2 4.3 %copy-start.16 = (s32[2,64,40]{1,2,0:T(8,128)S(1)}, s32[2,64,40]{1,2,0:T(8,128)}, u32[]{:S(2)}) copy-start(s32[2,64,40]{1,2,0:T(8,128)} %param.29) | copy-start | bytes 61444
  8.9 96.0 %copy-start.3 = (bf16[4096,256]{1,0:T(8,128)(2,1)}, bf16[4096,256]{1,0:T(8,128)(2,1)S(1)}, u32[]{:S(2)}) copy-start(bf16[4096,256]{1,0:T(8,128)(2,1)S(1)} %copy.87) | copy-start | bytes 6291460
  10.1 42.8 %copy-start.24 = (s32[2,128]{1,0:T(2,128)}, s32[2,128]{1,0:T(2,128)S(1)}, u32[]{:S(2)}) copy-start(s32[2,128]{1,0:T(2,128)S(1)} %get-tuple-element.82) | copy-start | bytes 3076
  11.8 2.6 copy-start.39
  14.6 33.9 %copy-start.43 = (s32[128]{0:T(128)}, s32[128]{0:T(128)S(1)}, u32[]{:S(2)}) copy-start(s32[128]{0:T(128)S(1)} %broadcast_in_dim.231) | copy-start | bytes 1540
  48.4 46.7 %all-to-all-start.1 = ((bf16[16,256,256]{2,1,0:T(8,128)(2,1)}), bf16[16,256,256]{2,1,0:T(8,128)(2,1)}, u32[]{:S(2)}, u32[]{:S(2)}) async-start(bf16[16,256,256]{2,1,0:T(8,128)(2,1)} %bitcast.130), calls=%async_computation.1 | async-start | bytes 4194304 | tf_op jit(solution)/shard_map/all_to_all | solution.py:102
  52.9 5.0 %copy-start.17 = (s32[2,64,40]{1,2,0:T(8,128)S(1)}, s32[2,64,40]{1,2,0:T(8,128)}, u32[]{:S(2)}) copy-start(s32[2,64,40]{1,2,0:T(8,128)} %param.30) | copy-start | bytes 61444
  57.9 6.4 %copy-start.21 = (bf16[128,512]{1,0:T(8,128)(2,1)S(1)}, bf16[128,512]{1,0:T(8,128)(2,1)}, u32[]{:S(2)}) copy-start(bf16[128,512]{1,0:T(8,128)(2,1)} %param.40) | copy-start | bytes 393220
  57.9 6.4 %copy-start.22 = (bf16[128,512]{1,0:T(8,128)(2,1)S(1)}, bf16[128,512]{1,0:T(8,128)(2,1)}, u32[]{:S(2)}) copy-start(bf16[128,512]{1,0:T(8,128)(2,1)} %param.39) | copy-start | bytes 393220
  58.5 6.9 %copy-start.26 = (f32[2,3,256]{2,0,1:T(2,128)S(1)}, f32[2,3,256]{2,0,1:T(2,128)}, u32[]{:S(2)}) copy-start(f32[2,3,256]{2,0,1:T(2,128)} %param.35) | copy-start | bytes 18436
  58.5 8.3 %copy-start.40 = (f32[128]{0:T(128)S(1)}, f32[128]{0:T(128)}, u32[]{:S(2)}) copy-start(f32[128]{0:T(128)} %param.32) | copy-start | bytes 1540
  61.2 4.2 %copy-start.48 = (s32[128]{0:T(128)}, s32[128]{0:T(128)S(1)}, u32[]{:S(2)}) copy-start(s32[128]{0:T(128)S(1)} %get-tuple-element.69) | copy-start | bytes 1540
  64.3 13.5 %copy-start.6 = (s32[4096]{0:T(1024)S(1)}, s32[4096]{0:T(1024)}, u32[]{:S(2)}) copy-start(s32[4096]{0:T(1024)} %param.22) | copy-start | bytes 49156
  65.4 39.5 %copy-start.12 = (s32[16,1,256]{2,1,0:T(1,128)S(1)}, s32[16,1,256]{2,1,0:T(1,128)}, u32[]{:S(2)}) copy-start(s32[16,1,256]{2,1,0:T(1,128)} %get-tuple-element.43) | copy-start | bytes 49156
  95.2 36.1 %all-to-all-start.2 = ((s32[16,1,32]{2,1,0:T(1,128)}), s32[16,1,32]{2,1,0:T(1,128)S(1)}, u32[]{:S(2)}, u32[]{:S(2)}) async-start(s32[16,1,32]{2,1,0:T(1,128)} %all_to_all.30), calls=%async_computation.2 | async-start | bytes 16384 | tf_op jit(solution)/shard_map/all_to_all | solution.py:102
  104.9 47.7 %all-gather.5.cloned.1.call-start = ((), (), s32[]{:S(2)}) async-start(), calls=%async_computation.6 | async-start | bytes 4325376 | tf_op jit(solution)/shard_map/all_gather | solution.py:251
  104.9 17.1 %copy-start.14 = (s32[3072]{0:T(1024)S(1)}, s32[3072]{0:T(1024)}, u32[]{:S(2)}) copy-start(s32[3072]{0:T(1024)} %pad_clamp_fusion.1) | copy-start | bytes 36868
  131.3 7.6 %copy-start.23 = (s32[2688]{0:T(1024)S(1)}, s32[2688]{0:T(1024)}, u32[]{:S(2)}) copy-start(s32[2688]{0:T(1024)} %pad_add_fusion.1) | copy-start | bytes 32260
  131.3 0.6 copy-start.19
  131.9 49.0 %all-to-all-start.4 = ((bf16[16,256,256]{2,1,0:T(8,128)(2,1)}), bf16[16,256,256]{2,1,0:T(8,128)(2,1)}, u32[]{:S(2)}, u32[]{:S(2)}) async-start(bf16[16,256,256]{2,1,0:T(8,128)(2,1)} %bitcast.19), calls=%async_computation.4 | async-start | bytes 4194304 | tf_op jit(solution)/shard_map/all_to_all | solution.py:102
  142.9 4.4 %copy-start.20 = (s32[16,1,32]{2,1,0:T(1,128)S(1)}, s32[16,1,32]{2,1,0:T(1,128)}, u32[]{:S(2)}) copy-start(s32[16,1,32]{2,1,0:T(1,128)} %copy-done.19) | copy-start | bytes 6148
  144.8 6.2 %copy-start.44 = (s32[128]{0:T(128)S(1)}, s32[128]{0:T(128)}, u32[]{:S(2)}) copy-start(s32[128]{0:T(128)} %copy-done.43) | copy-start | bytes 1540
  144.8 6.2 %copy-start.25 = (s32[2,128]{1,0:T(2,128)S(1)}, s32[2,128]{1,0:T(2,128)}, u32[]{:S(2)}) copy-start(s32[2,128]{1,0:T(2,128)} %copy-done.24) | copy-start | bytes 3076
  144.8 6.2 %copy-start.45 = (s32[128]{0:T(128)S(1)}, s32[128]{0:T(128)}, u32[]{:S(2)}) copy-start(s32[128]{0:T(128)} %broadcast_in_dim.245) | copy-start | bytes 1540
  144.8 6.8 %copy-start.41 = (f32[128]{0:T(128)S(1)}, f32[128]{0:T(128)}, u32[]{:S(2)}) copy-start(f32[128]{0:T(128)} %param.32) | copy-start | bytes 1540
  144.8 6.8 %copy-start.42 = (f32[128]{0:T(128)S(1)}, f32[128]{0:T(128)}, u32[]{:S(2)}) copy-start(f32[128]{0:T(128)} %param.31) | copy-start | bytes 1540
  145.8 7.8 %copy-start.7 = (bf16[512,3,256]{0,2,1:T(8,128)(2,1)S(1)}, bf16[512,3,256]{0,2,1:T(8,128)(2,1)}, u32[]{:S(2)}) copy-start(bf16[512,3,256]{0,2,1:T(8,128)(2,1)} %copy.66) | copy-start | bytes 2359300
  153.6 3.7 %copy-start.27 = (f32[1,1,256]{2,0,1:T(1,128)S(1)}, f32[1,1,256]{2,0,1:T(1,128)}, u32[]{:S(2)}) copy-start(f32[1,1,256]{2,0,1:T(1,128)} %get-tuple-element.53) | copy-start | bytes 3076
  153.6 3.7 %copy-start.29 = (f32[1,1,256]{2,0,1:T(1,128)S(1)}, f32[1,1,256]{2,0,1:T(1,128)}, u32[]{:S(2)}) copy-start(f32[1,1,256]{2,0,1:T(1,128)} %get-tuple-element.54) | copy-start | bytes 3076
  153.6 3.7 %copy-start.31 = (f32[1,1,256]{2,0,1:T(1,128)S(1)}, f32[1,1,256]{2,0,1:T(1,128)}, u32[]{:S(2)}) copy-start(f32[1,1,256]{2,0,1:T(1,128)} %get-tuple-element.55) | copy-start | bytes 3076
  153.6 3.7 %copy-start.33 = (f32[1,1,256]{2,0,1:T(1,128)S(1)}, f32[1,1,256]{2,0,1:T(1,128)}, u32[]{:S(2)}) copy-start(f32[1,1,256]{2,0,1:T(1,128)} %get-tuple-element.56) | copy-start | bytes 3076
  153.6 3.7 %copy-start.35 = (f32[1,1,256]{2,0,1:T(1,128)S(1)}, f32[1,1,256]{2,0,1:T(1,128)}, u32[]{:S(2)}) copy-start(f32[1,1,256]{2,0,1:T(1,128)} %get-tuple-element.57) | copy-start | bytes 3076
  153.6 3.7 %copy-start.37 = (f32[1,1,256]{2,0,1:T(1,128)S(1)}, f32[1,1,256]{2,0,1:T(1,128)}, u32[]{:S(2)}) copy-start(f32[1,1,256]{2,0,1:T(1,128)} %get-tuple-element.58) | copy-start | bytes 3076
  157.3 35.5 %copy-start.13 = (s32[2560]{0:T(1024)S(1)}, s32[2560]{0:T(1024)}, u32[]{:S(2)}) copy-start(s32[2560]{0:T(1024)} %get-tuple-element.21) | copy-start | bytes 30724
  157.3 35.6 %copy-start.50 = (s32[128]{0:T(128)S(1)}, s32[128]{0:T(128)}, u32[]{:S(2)}) copy-start(s32[128]{0:T(128)} %get-tuple-element.60) | copy-start | bytes 1540
  182.0 33.5 %all-to-all-start.3 = ((bf16[16,128,256]{2,1,0:T(8,128)(2,1)}), bf16[16,128,256]{2,1,0:T(8,128)(2,1)}, u32[]{:S(2)}, u32[]{:S(2)}) async-start(bf16[16,128,256]{2,1,0:T(8,128)(2,1)} %broadcast_in_dim.239), calls=%async_computation.3 | async-start | bytes 2097152 | tf_op jit(solution)/shard_map/all_to_all | solution.py:102
  191.8 49.0 %all-gather.7.cloned.1.call-start = ((), (), s32[]{:S(2)}) async-start(), calls=%async_computation.7 | async-start | bytes 4325376 | tf_op jit(solution)/shard_map/all_gather | solution.py:251
  192.8 2.7 copy-start.1
  195.6 5.4 %copy-start.10 = (bf16[512,512]{1,0:T(8,128)(2,1)S(1)}, bf16[512,512]{1,0:T(8,128)(2,1)}, u32[]{:S(2)}) copy-start(bf16[512,512]{1,0:T(8,128)(2,1)} %param.41) | copy-start | bytes 1572868
  241.8 1.8 copy-start.2
  243.7 5.8 %copy-start.8 = (bf16[1280,3,256]{0,2,1:T(8,128)(2,1)S(1)}, bf16[1280,3,256]{0,2,1:T(8,128)(2,1)}, u32[]{:S(2)}) copy-start(bf16[1280,3,256]{0,2,1:T(8,128)(2,1)} %copy.65) | copy-start | bytes 5898244
  243.7 5.8 %copy-start.18 = (bf16[128,128]{1,0:T(8,128)(2,1)S(1)}, bf16[128,128]{1,0:T(8,128)(2,1)}, u32[]{:S(2)}) copy-start(bf16[128,128]{1,0:T(8,128)(2,1)} %get-tuple-element.63) | copy-start | bytes 98308
  249.5 1.3 copy-start.28
  249.5 1.3 copy-start.30
  249.5 1.3 copy-start.32
  249.5 1.3 copy-start.34
  249.5 1.3 copy-start.36
  249.5 1.3 copy-start.38
  249.5 1.3 copy-start.49
  250.3 17.1 %copy-start.4 = (bf16[4096,256]{1,0:T(8,128)(2,1)S(1)}, bf16[4096,256]{1,0:T(8,128)(2,1)}, u32[]{:S(2)}) copy-start(bf16[4096,256]{1,0:T(8,128)(2,1)} %scatter_custom_fusion) | copy-start | bytes 6291460
  250.8 8.8 %copy-start.9 = (f32[128,512]{1,0:T(8,128)S(1)}, f32[128,512]{1,0:T(8,128)}, u32[]{:S(2)}) copy-start(f32[128,512]{1,0:T(8,128)} %all_gather.15) | copy-start | bytes 786436
  250.8 8.8 %copy-start.11 = (bf16[512,512]{1,0:T(8,128)(2,1)S(1)}, bf16[512,512]{1,0:T(8,128)(2,1)}, u32[]{:S(2)}) copy-start(bf16[512,512]{1,0:T(8,128)(2,1)} %param.41) | copy-start | bytes 1572868
  252.7 14.7 %all-to-all-start.5 = ((bf16[16,16,256]{2,1,0:T(8,128)(2,1)}), bf16[16,16,256]{2,1,0:T(8,128)(2,1)S(1)}, u32[]{:S(2)}, u32[]{:S(2)}) async-start(bf16[16,16,256]{2,1,0:T(8,128)(2,1)} %bitcast.142), calls=%async_computation.5 | async-start | bytes 262144 | tf_op jit(solution)/shard_map/all_to_all | solution.py:102
  270.1 1.3 copy-start.5
Sparse Core Ops, SparseCore 0:
  131.4 12.5 all-gather.4
  229.2 11.5 all-gather.6

commit v2 on v1

--- a/solution.py
+++ b/solution.py
@@ -100,6 +100,23 @@
 
 def exchange(x):
     return lax.all_to_all(x, "owner", split_axis=0, concat_axis=0, tiled=True)
+
+
+def gather_by_doubling(x, owners):
+    bit = owners // 2
+    while bit:
+        pairs = [(i, i ^ bit) for i in range(owners)]
+        x = jnp.concatenate([x, lax.ppermute(x, "owner", pairs)], axis=0)
+        bit //= 2
+    return x
+
+
+def place_by_doubling(owner, this, owners):
+    differ, place, bit, unit = owner ^ this, jnp.zeros_like(owner), owners // 2, 1
+    while bit:
+        place = place + jnp.where((differ & bit) != 0, unit, 0)
+        bit, unit = bit // 2, unit * 2
+    return place
 
 
 def write_rows(memory, rows, order, values):
@@ -193,8 +210,7 @@
 
     asked_ends = jnp.maximum(got[:, :, :cap] - 1, 0).reshape(-1)
     stamps = jnp.take(last_seen, asked_ends, mode="clip").reshape(owners, BATCHES * cap)
-    stamps = exchange(stamps).reshape(owners, BATCHES, cap).swapaxes(0, 1).reshape(BATCHES, -1)
-    base_seen = jnp.stack([jnp.take(stamps[b], end_pos[b], mode="clip") for b in range(BATCHES)])
+    stamps = exchange(stamps)
 
     def look(batch):
         rows = jnp.maximum(got[:, batch, :slots] - 1, 0).reshape(-1)
@@ -216,7 +232,10 @@
     near_code = time_code(time_two[:, None] - by_neighbor(nb_time), time_freq, time_phase)
     near_code = near_code.reshape(BATCHES, neighbors * points, -1)
 
-    first, second = exchange(look(0)), look(1)
+    looked, stamps = lax.optimization_barrier((look(0), stamps))
+    stamps = stamps.reshape(owners, BATCHES, cap).swapaxes(0, 1).reshape(BATCHES, -1)
+    base_seen = jnp.stack([jnp.take(stamps[b], end_pos[b], mode="clip") for b in range(BATCHES)])
+    first, second = exchange(looked), look(1)
     first, second, near_code, gru_in_flat, gru_hid_flat = lax.optimization_barrier(
         (first, second, near_code, gru_in_flat, gru_hid_flat)
     )
@@ -239,7 +258,8 @@
             index = jnp.where(written, best % total, 0)
             table, results[0] = lax.optimization_barrier((table, results[0]))
             table = jnp.concatenate([table, fresh_all], axis=0)
-            newer = owners * slots + index
+            block_of = place_by_doubling(index // points, owner_pos, owners)
+            newer = owners * slots + block_of * points + index % points
             pick_end = jnp.where(written[:points], newer[:points], pick_end)
             pick_near = jnp.where(written[points:], newer[points:], pick_near)
             since = jnp.take(all_meta[2], index[:points], mode="clip")
@@ -266,11 +286,14 @@
         update = jax.nn.sigmoid(block(from_msg, 1, 0) + block(from_mem, 1, 1))
         cand = jnp.tanh(block(from_msg, 2, 0) + reset * block(from_mem, 2, 1))
         fresh = ((1.0 - update) * cand + update * end_half).astype(BF)
+        query = jnp.dot(end_full, query_cols, preferred_element_type=F32)
+        query, fresh = lax.optimization_barrier((query, fresh))
         wrote = got[:, batch, :cap].reshape(-1) - 1
         order = got[:, batch, slots : slots + cap].reshape(-1)
         if batch + 1 < BATCHES:
-            fresh_all = exchange(jnp.broadcast_to(fresh, (owners, points, half))).reshape(total, half)
-            source = jnp.arange(owners, dtype=jnp.int32)[:, None] * points
+            fresh_all = gather_by_doubling(fresh, owners)
+            source = place_by_doubling(jnp.arange(owners, dtype=jnp.int32), owner_pos, owners)
+            source = source[:, None] * points
             source = source + got[:, batch, slots + cap :]
             values = jnp.take(fresh_all, source.reshape(-1), axis=0, mode="clip")
         else:
@@ -279,7 +302,6 @@
             values = exchange(sent.reshape(owners, cap, half)).reshape(-1, half)
         updated = write_rows(updated, wrote, order, values)
 
-        query = jnp.dot(end_full, query_cols, preferred_element_type=F32)
         attended = attend(full, near_code[batch], query, wide, twide, neighbors, scale)
         mixed = lax.all_gather(attended, "section", axis=1, tiled=True)
         emb = jnp.dot(mixed, own_cols, precision=lax.Precision.HIGHEST) + end_half

time: 280 us -> 264 us (0.943)
  blocking collectives: 20 us -> 4.2 us
  other arithmetic: 31.2 us -> 23.7 us
  starting transfers between devices: 37.8 us -> 45.1 us
  local copies, waits for them, and re-layouts: 96.4 us -> 103 us
  waiting for transfers between devices: 56 us -> 50.7 us
    all_to_all x5, waiting for transfers between devices: 52.5 us -> 4.06 us  [exchange(): return lax.all_to_all(x, 'owner', split_axis=0, concat_axis=0, tiled=True)]
    ppermute x0 -> x4, waiting for transfers between devices: none -> 46.5 us  [gather_by_doubling(): x = jnp.concatenate([x, lax.ppermute(x, 'owner', pairs)], axis=0)]
    all_to_all x1 -> x0, blocking collectives: 15.6 us -> none  [exchange(): return lax.all_to_all(x, 'owner', split_axis=0, concat_axis=0, tiled=True)]
    ppermute x0 -> x4, starting transfers between devices: none -> 6.43 us  [gather_by_doubling(): x = jnp.concatenate([x, lax.ppermute(x, 'owner', pairs)], axis=0)]
    unnamed x114 -> x77, local copies, waits for them, and re-layouts: 12.4 us -> 16.4 us
    all_gather x2, waiting for transfers between devices: 3.47 us -> 0.16 us  [on_device(): full = lax.all_gather(picked, 'section', axis=1, tiled=True)]
  transfers between devices with their start and end apart: 7 -> 11, of which waited for: 5 -> 7; matrix products, arithmetic and copies ran while one was open for 33% -> 35% of each run, Pallas kernels for 1% -> 3%
where the time goes in v2:
time: 264 us; the launch traced here: 263 us
  local copies, waits for them, and re-layouts  103 us (39%)
  waiting for transfers between devices  50.7 us (19%)
  starting transfers between devices  45.1 us (17%)
  other arithmetic  23.7 us (9%)
  between operations  15.2 us (6%)
  matrix products  14.3 us (5%)
  Pallas kernels  6.76 us (3%)
  blocking collectives  4.2 us (2%)
    ppermute x4, waiting for transfers between devices, gather_by_doubling(): x = jnp.concatenate([x, lax.ppermute(x, 'owner', pairs)], axis=0)  46.5 us
    all_to_all x5, starting transfers between devices, exchange(): return lax.all_to_all(x, 'owner', split_axis=0, concat_axis=0, tiled=True)  38.4 us
    gather x2, local copies, waits for them, and re-layouts, look(): jnp.take(memory, rows, axis=0, mode='clip').reshape(owners, slots, half)  34.1 us
    gather x2, local copies, waits for them, and re-layouts, on_device(): jnp.take(table, jnp.concatenate([pick_near, pick_end, pick_other]), axis=...  19 us
    unnamed x77, local copies, waits for them, and re-layouts  16.4 us
    scatter x2, local copies, waits for them, and re-layouts, write_rows(): return memory.at[place].set(values, mode='drop')  11.9 us
    convert_element_type x2, other arithmetic, time_code(): return jnp.cos(angle).astype(BF)  11.2 us
    pallas_call x2, Pallas kernels, attend(): pl.pallas_call(functools.partial(attend_kernel, scale, group), out_shape=...  6.76 us
  transfers between devices with their start and end apart: 11, of which 7 were waited for; matrix products, arithmetic and copies ran while one was open for 35% of the time, Pallas kernels for 3%

profile of v2, /device:TPU:0, one launch (start us, length us, event | category | flops | bytes accessed | tf_op | source)
XLA Modules:
  0.0 262.9 jit_solution(1541324466398530237)
XLA Ops:
  7.2 1.7 copy.96
  12.3 0.9 fusion
  13.2 0.9 fusion.11
  15.0 0.7 copy.62
  15.7 8.3 %all-to-all-start = ((s32[16,1,960]{2,1,0:T(1,128)}), s32[16,1,960]{2,1,0:T(1,128)S(1)}, u32[]{:S(2)}, u32[]{:S(2)}) async-start(s32[16,1,960]{2,1,0:T(1,128)} %copy.62), calls=%async_computation | async-start | bytes 131072 | tf_op jit(solution)/shard_map/all_to_all | solution.py:102
  24.6 4.1 %copy.65 = bf16[1280,3,256]{0,2,1:T(8,128)(2,1)} copy(bf16[1280,3,256]{2,0,1:T(8,128)(2,1)} %param.33) | data formatting | bytes 3932160 | tf_op args[12]
  28.7 2.3 copy.66
  31.8 3.1 %gather_fusion.1 = s32[512]{0:T(512)S(1)} fusion(s32[4096]{0:T(1024)S(1)} %copy-done.4, s32[1024]{0:T(1024)S(1)} %pad_clamp_fusion.6), kind=kCustom, calls=%fused_computation.1 | custom fusion | bytes 6144 | tf_op jit(solution)/shard_map/jit(_take)/gather | solution.py:212
  35.0 0.7 all_to_all.28
  35.7 6.4 %all-to-all-start.1 = ((s32[16,1,32]{2,1,0:T(1,128)}), s32[16,1,32]{2,1,0:T(1,128)S(1)}, u32[]{:S(2)}, u32[]{:S(2)}) async-start(s32[16,1,32]{2,1,0:T(1,128)} %all_to_all.28), calls=%async_computation.1 | async-start | bytes 16384 | tf_op jit(solution)/shard_map/all_to_all | solution.py:102
  42.1 17.1 %gather_fusion = bf16[4096,256]{1,0:T(8,128)(2,1)} fusion(bf16[4096,256]{1,0:T(8,128)(2,1)S(1)} %copy.96, s32[4096]{0:T(1024)S(1)} %broadcast_clamp_fusion.1), kind=kCustom, calls=%fused_computation | custom fusion | bytes 4210688 | tf_op jit(solution)/shard_map/jit(_take)/gather | solution.py:217
  59.2 7.1 %all-to-all-start.2 = ((bf16[16,256,256]{2,1,0:T(8,128)(2,1)}), bf16[16,256,256]{2,1,0:T(8,128)(2,1)}, u32[]{:S(2)}, u32[]{:S(2)}) async-start(bf16[16,256,256]{2,1,0:T(8,128)(2,1)} %bitcast.131), calls=%async_computation.2 | async-start | bytes 4194304 | tf_op jit(solution)/shard_map/all_to_all | solution.py:102
  67.0 0.6 broadcast_in_dim.273
  69.2 1.1 constant_dynamic-slice_fusion.2
  70.3 1.4 fusion.195
  71.7 0.7 slice_bitcast_fusion.2
  72.4 10.7 %cosine_convert_fusion = bf16[2,2560,128]{2,1,0:T(8,128)(2,1)} fusion(f32[128]{0:T(128)} %param.32, f32[128]{0:T(128)} %param.31, f32[2,2560]{1,0:T(2,128)S(1)} %bitcast.145), kind=kLoop, calls=%fused_computation.15 | loop fusion | flops 1966080 | bytes 1332224 | tf_op jit(solution)/shard_map/convert_element_type | solution.py:19
  83.2 17.0 %gather_fusion.2 = bf16[4096,256]{1,0:T(8,128)(2,1)} fusion(bf16[4096,256]{1,0:T(8,128)(2,1)S(1)} %copy.96, s32[4096]{0:T(1024)S(1)} %broadcast_clamp_fusion), kind=kCustom, calls=%fused_computation.2 | custom fusion | bytes 4210688 | tf_op jit(solution)/shard_map/jit(_take)/gather | solution.py:217
  100.3 4.0 %select_reduce_fusion = s32[2688]{0:T(1024)S(1)} fusion(s32[2048]{0:T(1024)S(1)} %bitcast.166, s32[2688]{0:T(1024)S(1)} %pad_add_fusion.1, s32[2048]{0:T(1024)S(1)} %bitcast.167), kind=kLoop, calls=%fused_computation.11 | loop fusion | flops 16512384 | bytes 37888 | tf_op jit(solution)/shard_map/reduce_max | solution.py:254
  105.0 3.6 %all-to-all-done.2 = bf16[16,256,256]{2,1,0:T(8,128)(2,1)} async-done(((bf16[16,256,256]{2,1,0:T(8,128)(2,1)}), bf16[16,256,256]{2,1,0:T(8,128)(2,1)}, u32[]{:S(2)}, u32[]{:S(2)}) %all-to-all-start.2) | async-done | bytes 2097184 | tf_op jit(solution)/shard_map/all_to_all | solution.py:102
  108.5 9.3 %gather_fusion.3 = bf16[2816,256]{1,0:T(8,128)(2,1)} fusion(bf16[4096,256]{1,0:T(8,128)(2,1)} %bitcast.24, s32[3072]{0:T(1024)S(1)} %pad_clamp_fusion.1), kind=kCustom, calls=%fused_computation.3 | custom fusion | bytes 2894848 | tf_op jit(solution)/shard_map/jit(_take)/gather | solution.py:268
  117.8 1.0 and_compare_fusion
  119.3 1.1 gather_fusion.6
  120.5 9.8 %all-to-all-start.3 = ((bf16[16,256,256]{2,1,0:T(8,128)(2,1)}), bf16[16,256,256]{2,1,0:T(8,128)(2,1)}, u32[]{:S(2)}, u32[]{:S(2)}) async-start(bf16[16,256,256]{2,1,0:T(8,128)(2,1)} %bitcast.20), calls=%async_computation.3 | async-start | bytes 4194304 | tf_op jit(solution)/shard_map/all_to_all | solution.py:102
  130.7 1.5 gather_fusion.7
  132.2 1.4 gather_fusion.4
  134.3 1.2 fusion.46.query
  135.5 1.0 fusion.193
  136.5 1.3 fusion.188
  137.9 0.8 fusion.25
  138.7 1.1 fusion.57
  139.8 2.8 %collective-permute-start = (bf16[128,256]{1,0:T(8,128)(2,1)S(1)}, bf16[128,256]{1,0:T(8,128)(2,1)S(1)}, u32[]{:S(2)}, u32[]{:S(2)}) collective-permute-start(bf16[128,256]{1,0:T(8,128)(2,1)S(1)} %fusion.57), channel_id=1, source_target_pairs={{0,16},{2,18},{4,20},{6,22},{8,24},{10,26},{12,28},{14,30},{16,0},... | collective-permute-start | bytes 196616 | tf_op jit(solution)/shard_map/ppermute | solution.py:109
  142.7 37.7 %collective-permute-done = bf16[128,256]{1,0:T(8,128)(2,1)S(1)} collective-permute-done((bf16[128,256]{1,0:T(8,128)(2,1)S(1)}, bf16[128,256]{1,0:T(8,128)(2,1)S(1)}, u32[]{:S(2)}, u32[]{:S(2)}) %collective-permute-start) | collective-permute-done | bytes 65568 | tf_op jit(solution)/shard_map/ppermute | solution.py:109
  180.6 3.4 %shard_map.212 = f32[128,256]{1,0:T(8,128)S(1)} custom-call(bf16[2816,512]{1,0:T(8,128)(2,1)S(1)} %copy-done.1, bf16[2560,128]{1,0:T(8,128)(2,1)S(1)} %get-tuple-element.53.code, f32[128,256]{1,0:T(8,128)S(1)} %fusion.46.query, bf16[512,512]{1,0:T(8,128)(2,1)S(1)} %pad_maximum_fusion.1.wide, bf16[128,512]{1,0:T(8,128)(2,1)S(1)} %pad_maximum_fusion.4.twide), custom_call_target="tpu_custom_call" | custom-call | flops 1677721600 | bytes 3801088 | tf_op jit(solution)/shard_map/pallas_call | solution.py:79
  184.0 1.5 collective-permute-done.1
  185.5 0.7 pad_maximum_fusion.2
  186.2 2.4 collective-permute-start.2
  188.6 2.2 all_gather.13
  190.8 1.1 fusion.7
  192.0 1.2 collective-permute-done.2
  193.2 0.8 pad_maximum_fusion
  194.0 1.1 collective-permute-start.3
  195.1 3.1 %constant_dynamic-update-slice_fusion.10 = bf16[6144,256]{1,0:T(8,128)(2,1)} fusion(bf16[4096,256]{1,0:T(8,128)(2,1)} %bitcast.39), kind=kLoop, calls=%fused_computation.198 | loop fusion | bytes 4194304
  198.2 0.7 constant_dynamic-update-slice_fusion.9
  198.8 0.7 constant_dynamic-update-slice_fusion.8
  199.5 0.7 constant_dynamic-update-slice_fusion.7
  200.2 0.9 constant_dynamic-update-slice_fusion.6
  201.1 6.1 %collective-permute-done.3 = bf16[1024,256]{1,0:T(8,128)(2,1)} collective-permute-done((bf16[1024,256]{1,0:T(8,128)(2,1)}, bf16[1024,256]{1,0:T(8,128)(2,1)}, u32[]{:S(2)}, u32[]{:S(2)}) %collective-permute-start.3) | collective-permute-done | bytes 524320 | tf_op jit(solution)/shard_map/ppermute | solution.py:109
  207.1 2.1 constant_dynamic-update-slice_fusion.5
  209.3 9.7 %gather_fusion.5 = bf16[2816,256]{1,0:T(8,128)(2,1)} fusion(bf16[6144,256]{1,0:T(8,128)(2,1)} %get-tuple-element.58, s32[3072]{0:T(1024)S(1)} %pad_clamp_fusion), kind=kCustom, calls=%fused_computation.6 | custom fusion | bytes 2894848 | tf_op jit(solution)/shard_map/jit(_take)/gather | solution.py:268
  220.4 7.1 %scatter_custom_fusion = bf16[4096,256]{1,0:T(8,128)(2,1)} fusion(bf16[4096,256]{1,0:T(8,128)(2,1)} %copy-done.3, s32[256]{0:T(256)S(1)} %bitcast.170, bf16[2048,256]{1,0:T(8,128)(2,1)} %get-tuple-element.59, s32[1024]{0:T(1024)S(1)} %pad_clamp_fusion.4), kind=kCustom, calls=%fused_computation.156 | custom fusion | bytes 2097152 | tf_op jit(solution)/shard_map/scatter | solution.py:126
  227.7 1.0 fusion.192
  228.7 2.3 fusion.33
  231.0 1.3 fusion.185
  232.3 1.0 fusion.59
  233.3 1.1 fusion.44.query
  234.4 0.8 convolution_convert_fusion
  235.2 6.8 %all-to-all-start.4 = ((bf16[16,16,256]{2,1,0:T(8,128)(2,1)}), bf16[16,16,256]{2,1,0:T(8,128)(2,1)S(1)}, u32[]{:S(2)}, u32[]{:S(2)}) async-start(bf16[16,16,256]{2,1,0:T(8,128)(2,1)} %bitcast.49), calls=%async_computation.4 | async-start | bytes 262144 | tf_op jit(solution)/shard_map/all_to_all | solution.py:102
  242.1 1.8 copy-done.2
  243.9 3.4 %shard_map.213 = f32[128,256]{1,0:T(8,128)S(1)} custom-call(bf16[2816,512]{1,0:T(8,128)(2,1)S(1)} %copy-done.2, bf16[2560,128]{1,0:T(8,128)(2,1)S(1)} %get-tuple-element.52.code, f32[128,256]{1,0:T(8,128)S(1)} %fusion.44.query, bf16[512,512]{1,0:T(8,128)(2,1)S(1)} %pad_maximum_fusion.1.wide, bf16[128,512]{1,0:T(8,128)(2,1)S(1)} %pad_maximum_fusion.4.twide), custom_call_target="tpu_custom_call" | custom-call | flops 1677721600 | bytes 3801088 | tf_op jit(solution)/shard_map/pallas_call | solution.py:79
  247.3 2.0 all_gather.15
  249.3 1.1 fusion.8
  250.4 0.8 pad_maximum_fusion.5
  251.3 4.8 %scatter_fusion = bf16[4096,256]{1,0:T(8,128)(2,1)} fusion(bf16[4096,256]{1,0:T(8,128)(2,1)} %scatter_custom_fusion, s32[256]{0:T(256)S(1)} %bitcast.168, bf16[256,256]{1,0:T(8,128)(2,1)S(1)} %bitcast.136), kind=kCustom, calls=%fused_computation.10 | custom fusion | bytes 394240 | tf_op jit(solution)/shard_map/scatter | solution.py:126
  (203 shorter events, 11.6 us)
Async XLA Ops:
  7.2 127.1 %copy-start = (bf16[512,512]{1,0:T(8,128)(2,1)S(1)}, bf16[512,512]{1,0:T(8,128)(2,1)}, u32[]{:S(2)}) copy-start(bf16[512,512]{1,0:T(8,128)(2,1)} %param.36) | copy-start | bytes 1572868
  7.2 1.8 copy-start.28
  7.2 2.6 copy-start.29
  7.2 2.4 copy-start.30
  7.2 3.2 %copy-start.10 = (s32[2,64,40,1]{1,3,2,0:T(1,128)S(1)}, s32[2,64,40,1]{1,3,2,0:T(1,128)}, u32[]{:S(2)}) copy-start(s32[2,64,40,1]{1,3,2,0:T(1,128)} %param.28) | copy-start | bytes 61444
  7.2 4.2 %copy-start.11 = (s32[2,64,40]{1,2,0:T(8,128)S(1)}, s32[2,64,40]{1,2,0:T(8,128)}, u32[]{:S(2)}) copy-start(s32[2,64,40]{1,2,0:T(8,128)} %param.29) | copy-start | bytes 61444
  8.9 74.3 %copy-start.3 = (bf16[4096,256]{1,0:T(8,128)(2,1)}, bf16[4096,256]{1,0:T(8,128)(2,1)S(1)}, u32[]{:S(2)}) copy-start(bf16[4096,256]{1,0:T(8,128)(2,1)S(1)} %copy.96) | copy-start | bytes 6291460
  10.2 56.2 %copy-start.18 = (s32[2,128]{1,0:T(2,128)}, s32[2,128]{1,0:T(2,128)S(1)}, u32[]{:S(2)}) copy-start(s32[2,128]{1,0:T(2,128)S(1)} %get-tuple-element.108) | copy-start | bytes 3076
  11.6 2.7 %copy-start.22 = (s32[2,64]{1,0:T(2,128)S(1)}, s32[2,64]{1,0:T(2,128)}, u32[]{:S(2)}) copy-start(s32[2,64]{1,0:T(2,128)} %param.26) | copy-start | bytes 1540
  12.3 11.7 %copy-start.12 = (s32[2,64,40]{1,2,0:T(8,128)S(1)}, s32[2,64,40]{1,2,0:T(8,128)}, u32[]{:S(2)}) copy-start(s32[2,64,40]{1,2,0:T(8,128)} %param.30) | copy-start | bytes 61444
  14.6 9.6 %copy-start.25 = (s32[128]{0:T(128)}, s32[128]{0:T(128)S(1)}, u32[]{:S(2)}) copy-start(s32[128]{0:T(128)S(1)} %broadcast_in_dim.256) | copy-start | bytes 1540
  15.7 15.9 %all-to-all-start = ((s32[16,1,960]{2,1,0:T(1,128)}), s32[16,1,960]{2,1,0:T(1,128)S(1)}, u32[]{:S(2)}, u32[]{:S(2)}) async-start(s32[16,1,960]{2,1,0:T(1,128)} %copy.62), calls=%async_computation | async-start | bytes 131072 | tf_op jit(solution)/shard_map/all_to_all | solution.py:102
  24.6 7.2 %copy-start.4 = (s32[4096]{0:T(1024)S(1)}, s32[4096]{0:T(1024)}, u32[]{:S(2)}) copy-start(s32[4096]{0:T(1024)} %param.22) | copy-start | bytes 49156
  35.7 23.5 %all-to-all-start.1 = ((s32[16,1,32]{2,1,0:T(1,128)}), s32[16,1,32]{2,1,0:T(1,128)S(1)}, u32[]{:S(2)}, u32[]{:S(2)}) async-start(s32[16,1,32]{2,1,0:T(1,128)} %all_to_all.28), calls=%async_computation.1 | async-start | bytes 16384 | tf_op jit(solution)/shard_map/all_to_all | solution.py:102
  59.1 10.0 %copy-start.13 = (bf16[128,512]{1,0:T(8,128)(2,1)S(1)}, bf16[128,512]{1,0:T(8,128)(2,1)}, u32[]{:S(2)}) copy-start(bf16[128,512]{1,0:T(8,128)(2,1)} %param.40) | copy-start | bytes 393220
  59.1 10.0 %copy-start.14 = (bf16[128,512]{1,0:T(8,128)(2,1)S(1)}, bf16[128,512]{1,0:T(8,128)(2,1)}, u32[]{:S(2)}) copy-start(bf16[128,512]{1,0:T(8,128)(2,1)} %param.39) | copy-start | bytes 393220
  59.2 49.4 %all-to-all-start.2 = ((bf16[16,256,256]{2,1,0:T(8,128)(2,1)}), bf16[16,256,256]{2,1,0:T(8,128)(2,1)}, u32[]{:S(2)}, u32[]{:S(2)}) async-start(bf16[16,256,256]{2,1,0:T(8,128)(2,1)} %bitcast.131), calls=%async_computation.2 | async-start | bytes 4194304 | tf_op jit(solution)/shard_map/all_to_all | solution.py:102
  66.3 68.0 %all-gather.5.cloned.1.call-start = ((), (), s32[]{:S(2)}) async-start(), calls=%async_computation.5 | async-start | bytes 4325376 | tf_op jit(solution)/shard_map/all_gather | solution.py:271
  67.8 2.5 copy-start.20
  120.4 13.2 %copy-start.19 = (s32[2,128]{1,0:T(2,128)S(1)}, s32[2,128]{1,0:T(2,128)}, u32[]{:S(2)}) copy-start(s32[2,128]{1,0:T(2,128)} %copy-done.18) | copy-start | bytes 3076
  120.4 13.2 %copy-start.27 = (s32[128]{0:T(128)S(1)}, s32[128]{0:T(128)}, u32[]{:S(2)}) copy-start(s32[128]{0:T(128)} %broadcast_in_dim.273) | copy-start | bytes 1540
  120.4 13.2 %copy-start.26 = (s32[128]{0:T(128)S(1)}, s32[128]{0:T(128)}, u32[]{:S(2)}) copy-start(s32[128]{0:T(128)} %copy-done.25) | copy-start | bytes 1540
  120.5 13.2 %copy-start.23 = (f32[128]{0:T(128)S(1)}, f32[128]{0:T(128)}, u32[]{:S(2)}) copy-start(f32[128]{0:T(128)} %param.32) | copy-start | bytes 1540
  120.5 13.2 %copy-start.24 = (f32[128]{0:T(128)S(1)}, f32[128]{0:T(128)}, u32[]{:S(2)}) copy-start(f32[128]{0:T(128)} %param.31) | copy-start | bytes 1540
  120.5 74.6 %all-to-all-start.3 = ((bf16[16,256,256]{2,1,0:T(8,128)(2,1)}), bf16[16,256,256]{2,1,0:T(8,128)(2,1)}, u32[]{:S(2)}, u32[]{:S(2)}) async-start(bf16[16,256,256]{2,1,0:T(8,128)(2,1)} %bitcast.20), calls=%async_computation.3 | async-start | bytes 4194304 | tf_op jit(solution)/shard_map/all_to_all | solution.py:102
  130.3 6.2 %copy-start.5 = (bf16[512,3,256]{0,2,1:T(8,128)(2,1)S(1)}, bf16[512,3,256]{0,2,1:T(8,128)(2,1)}, u32[]{:S(2)}) copy-start(bf16[512,3,256]{0,2,1:T(8,128)(2,1)} %copy.66) | copy-start | bytes 2359300
  130.3 97.4 %all-gather.7.cloned.1.call-start = ((), (), s32[]{:S(2)}) async-start(), calls=%async_computation.6 | async-start | bytes 4325376 | tf_op jit(solution)/shard_map/all_gather | solution.py:271
  134.2 3.6 %copy-start.7 = (bf16[1280,3,256]{0,2,1:T(8,128)(2,1)S(1)}, bf16[1280,3,256]{0,2,1:T(8,128)(2,1)}, u32[]{:S(2)}) copy-start(bf16[1280,3,256]{0,2,1:T(8,128)(2,1)} %copy.65) | copy-start | bytes 5898244
  136.5 2.2 copy-start.15
  136.5 2.2 copy-start.16
  136.5 2.2 copy-start.17
  137.8 4.8 %copy-start.6 = (bf16[2,2560,128]{2,1,0:T(8,128)(2,1)S(1)}, bf16[2,2560,128]{2,1,0:T(8,128)(2,1)}, u32[]{:S(2)}) copy-start(bf16[2,2560,128]{2,1,0:T(8,128)(2,1)} %cosine_convert_fusion) | copy-start | bytes 3932164
  138.7 41.9 %copy-start.1 = (bf16[2816,512]{1,0:T(8,128)(2,1)S(1)}, bf16[2816,512]{1,0:T(8,128)(2,1)}, u32[]{:S(2)}) copy-start(bf16[2816,512]{1,0:T(8,128)(2,1)} %all-gather.5.cloned.1.call-done.near) | copy-start | bytes 8650756
  139.8 40.6 %collective-permute-start = (bf16[128,256]{1,0:T(8,128)(2,1)S(1)}, bf16[128,256]{1,0:T(8,128)(2,1)S(1)}, u32[]{:S(2)}, u32[]{:S(2)}) collective-permute-start(bf16[128,256]{1,0:T(8,128)(2,1)S(1)} %fusion.57), channel_id=1, source_target_pairs={{0,16},{2,18},{4,20},{6,22},{8,24},{10,26},{12,28},{14,30},{16,0},... | collective-permute-start | bytes 196616 | tf_op jit(solution)/shard_map/ppermute | solution.py:109
  180.5 5.0 %collective-permute-start.1 = (bf16[256,256]{1,0:T(8,128)(2,1)S(1)}, bf16[256,256]{1,0:T(8,128)(2,1)S(1)}, u32[]{:S(2)}, u32[]{:S(2)}) collective-permute-start(bf16[256,256]{1,0:T(8,128)(2,1)S(1)} %pad_maximum_fusion.3), channel_id=1, source_target_pairs={{0,8},{2,10},{4,12},{6,14},{8,0},{10,2},{12,4},{14,6},{16,24},{18,... | collective-permute-start | bytes 393224 | tf_op jit(solution)/shard_map/ppermute | solution.py:109
  180.6 10.3 %copy-start.8 = (bf16[512,512]{1,0:T(8,128)(2,1)S(1)}, bf16[512,512]{1,0:T(8,128)(2,1)}, u32[]{:S(2)}) copy-start(bf16[512,512]{1,0:T(8,128)(2,1)} %param.41) | copy-start | bytes 1572868
  186.2 7.0 %collective-permute-start.2 = (bf16[512,256]{1,0:T(8,128)(2,1)}, bf16[512,256]{1,0:T(8,128)(2,1)S(1)}, u32[]{:S(2)}, u32[]{:S(2)}) collective-permute-start(bf16[512,256]{1,0:T(8,128)(2,1)} %pad_maximum_fusion.2), channel_id=1, source_target_pairs={{0,4},{2,6},{4,0},{6,2},{8,12},{10,14},{12,8},{14,10},{16,20},{18,... | collective-permute-start | bytes 786440 | tf_op jit(solution)/shard_map/ppermute | solution.py:109
  194.0 13.1 %collective-permute-start.3 = (bf16[1024,256]{1,0:T(8,128)(2,1)}, bf16[1024,256]{1,0:T(8,128)(2,1)}, u32[]{:S(2)}, u32[]{:S(2)}) collective-permute-start(bf16[1024,256]{1,0:T(8,128)(2,1)} %pad_maximum_fusion), channel_id=1, source_target_pairs={{0,2},{2,0},{4,6},{6,4},{8,10},{10,8},{12,14},{14,12},{16,18},{18,... | collective-permute-start | bytes 1572872 | tf_op jit(solution)/shard_map/ppermute | solution.py:109
  231.0 3.4 %copy-start.21 = (s32[128]{0:T(128)S(1)}, s32[128]{0:T(128)}, u32[]{:S(2)}) copy-start(s32[128]{0:T(128)} %copy-done.20) | copy-start | bytes 1540
  235.2 16.0 %all-to-all-start.4 = ((bf16[16,16,256]{2,1,0:T(8,128)(2,1)}), bf16[16,16,256]{2,1,0:T(8,128)(2,1)S(1)}, u32[]{:S(2)}, u32[]{:S(2)}) async-start(bf16[16,16,256]{2,1,0:T(8,128)(2,1)} %bitcast.49), calls=%async_computation.4 | async-start | bytes 262144 | tf_op jit(solution)/shard_map/all_to_all | solution.py:102
  242.1 1.8 copy-start.2
  243.9 5.4 %copy-start.9 = (bf16[512,512]{1,0:T(8,128)(2,1)S(1)}, bf16[512,512]{1,0:T(8,128)(2,1)}, u32[]{:S(2)}) copy-start(bf16[512,512]{1,0:T(8,128)(2,1)} %param.41) | copy-start | bytes 1572868
Sparse Core Ops, SparseCore 0:
  117.9 15.4 all-gather.4
  219.1 8.5 all-gather.6

commit v3 on v2

--- a/solution.py
+++ b/solution.py
@@ -239,7 +239,7 @@
     first, second, near_code, gru_in_flat, gru_hid_flat = lax.optimization_barrier(
         (first, second, near_code, gru_in_flat, gru_hid_flat)
     )
-    came = [first.reshape(-1, half), exchange(second).reshape(-1, half)]
+    came = [first.reshape(-1, half)]
 
     results = []
     updated = memory
@@ -292,6 +292,8 @@
         order = got[:, batch, slots : slots + cap].reshape(-1)
         if batch + 1 < BATCHES:
             fresh_all = gather_by_doubling(fresh, owners)
+            second, fresh_all = lax.optimization_barrier((second, fresh_all))
+            came.append(exchange(second).reshape(-1, half))
             source = place_by_doubling(jnp.arange(owners, dtype=jnp.int32), owner_pos, owners)
             source = source[:, None] * points
             source = source + got[:, batch, slots + cap :]

time: 264 us -> 287 us (1.087)
  blocking collectives: 4.2 us -> 19.9 us
  other arithmetic: 23.7 us -> 35 us
  starting transfers between devices: 45.1 us -> 37.1 us
  waiting for transfers between devices: 50.7 us -> 56.5 us
    ppermute x4, waiting for transfers between devices: 46.5 us -> 16.5 us  [gather_by_doubling(): x = jnp.concatenate([x, lax.ppermute(x, 'owner', pairs)], axis=0)]
    all_to_all x5 -> x4, waiting for transfers between devices: 4.06 us -> 31.5 us  [exchange(): return lax.all_to_all(x, 'owner', split_axis=0, concat_axis=0, tiled=True)]
    all_to_all x0 -> x1, blocking collectives: none -> 15.6 us  [exchange(): return lax.all_to_all(x, 'owner', split_axis=0, concat_axis=0, tiled=True)]
    all_to_all x5 -> x4, starting transfers between devices: 38.4 us -> 27.6 us  [exchange(): return lax.all_to_all(x, 'owner', split_axis=0, concat_axis=0, tiled=True)]
    all_gather x2, waiting for transfers between devices: 0.16 us -> 8.46 us  [on_device(): full = lax.all_gather(picked, 'section', axis=1, tiled=True)]
    concatenate x0 -> x1, other arithmetic: none -> 3.75 us  [on_device(): table = jnp.concatenate([table, fresh_all], axis=0)]
    ppermute x4, starting transfers between devices: 6.43 us -> 9.3 us  [gather_by_doubling(): x = jnp.concatenate([x, lax.ppermute(x, 'owner', pairs)], axis=0)]
    unnamed x77 -> x104, local copies, waits for them, and re-layouts: 16.4 us -> 13.7 us
  transfers between devices with their start and end apart: 11 -> 10, of which waited for: 7 -> 8; matrix products, arithmetic and copies ran while one was open for 35% -> 33% of each run, Pallas kernels for 3% -> 1%
where the time goes in v3:
time: 287 us; the launch traced here: 285 us
  local copies, waits for them, and re-layouts  102 us (36%)
  waiting for transfers between devices  56.5 us (20%)
  starting transfers between devices  37.1 us (13%)
  other arithmetic  35 us (12%)
  blocking collectives  19.9 us (7%)
  between operations  15.1 us (5%)
  matrix products  12.4 us (4%)
  Pallas kernels  6.76 us (2%)
    gather x2, local copies, waits for them, and re-layouts, look(): jnp.take(memory, rows, axis=0, mode='clip').reshape(owners, slots, half)  33.9 us
    all_to_all x4, waiting for transfers between devices, exchange(): return lax.all_to_all(x, 'owner', split_axis=0, concat_axis=0, tiled=True)  31.5 us
    all_to_all x4, starting transfers between devices, exchange(): return lax.all_to_all(x, 'owner', split_axis=0, concat_axis=0, tiled=True)  27.6 us
    gather x2, local copies, waits for them, and re-layouts, on_device(): jnp.take(table, jnp.concatenate([pick_near, pick_end, pick_other]), axis=...  19.4 us
    ppermute x4, waiting for transfers between devices, gather_by_doubling(): x = jnp.concatenate([x, lax.ppermute(x, 'owner', pairs)], axis=0)  16.5 us
    all_to_all x1, blocking collectives, exchange(): return lax.all_to_all(x, 'owner', split_axis=0, concat_axis=0, tiled=True)  15.6 us
    unnamed x104, local copies, waits for them, and re-layouts  13.7 us
    convert_element_type x2, other arithmetic, time_code(): return jnp.cos(angle).astype(BF)  12.4 us
  transfers between devices with their start and end apart: 10, of which 8 were waited for; matrix products, arithmetic and copies ran while one was open for 33% of the time, Pallas kernels for 1%

profile of v3, /device:TPU:0, one launch (start us, length us, event | category | flops | bytes accessed | tf_op | source)
XLA Modules:
  0.0 284.9 jit_solution(8611684665054306760)
XLA Ops:
  7.2 1.7 copy.91
  13.5 0.9 fusion
  14.4 0.9 fusion.11
  16.7 15.6 %all_to_all.39 = s32[16,1,960]{2,1,0:T(1,128)S(1)} all-to-all(s32[16,1,960]{2,1,0:T(1,128)S(1)} %copy.62), channel_id=1, replica_groups=mesh['owner'=16,'section'=2] {'owner'}, dimensions={0} | all-to-all | bytes 122880 | tf_op jit(solution)/shard_map/all_to_all | solution.py:102
  33.3 3.1 %gather_fusion.1 = s32[512]{0:T(512)S(1)} fusion(s32[4096]{0:T(1024)S(1)} %copy-done.4, s32[1024]{0:T(1024)S(1)} %pad_clamp_fusion.6), kind=kCustom, calls=%fused_computation.1 | custom fusion | bytes 6144 | tf_op jit(solution)/shard_map/jit(_take)/gather | solution.py:212
  37.1 3.5 %all-to-all-start.1 = ((s32[16,1,32]{2,1,0:T(1,128)}), s32[16,1,32]{2,1,0:T(1,128)S(1)}, u32[]{:S(2)}, u32[]{:S(2)}) async-start(s32[16,1,32]{2,1,0:T(1,128)} %all_to_all.28), calls=%async_computation.1 | async-start | bytes 16384 | tf_op jit(solution)/shard_map/all_to_all | solution.py:102
  40.6 17.0 %gather_fusion = bf16[4096,256]{1,0:T(8,128)(2,1)} fusion(bf16[4096,256]{1,0:T(8,128)(2,1)S(1)} %copy.91, s32[4096]{0:T(1024)S(1)} %broadcast_clamp_fusion.1), kind=kCustom, calls=%fused_computation | custom fusion | bytes 4210688 | tf_op jit(solution)/shard_map/jit(_take)/gather | solution.py:217
  58.1 6.9 %all-to-all-start.2 = ((bf16[16,256,256]{2,1,0:T(8,128)(2,1)}), bf16[16,256,256]{2,1,0:T(8,128)(2,1)}, u32[]{:S(2)}, u32[]{:S(2)}) async-start(bf16[16,256,256]{2,1,0:T(8,128)(2,1)} %bitcast.132), calls=%async_computation.2 | async-start | bytes 4194304 | tf_op jit(solution)/shard_map/all_to_all | solution.py:102
  66.1 4.0 %copy.65 = bf16[1280,3,256]{0,2,1:T(8,128)(2,1)} copy(bf16[1280,3,256]{2,0,1:T(8,128)(2,1)} %param.33) | data formatting | bytes 3932160 | tf_op args[12]
  71.3 1.4 copy.66
  72.8 1.1 slice_reduce_fusion.7
  73.8 0.8 reshape_squeeze.12
  75.3 0.9 reshape.576
  77.5 1.5 slice_reduce_fusion
  80.2 10.8 %cosine_convert_fusion = bf16[2,2560,128]{2,1,0:T(8,128)(2,1)} fusion(f32[128]{0:T(128)} %param.32, f32[128]{0:T(128)} %param.31, f32[2,2560]{1,0:T(2,128)} %bitcast.146), kind=kLoop, calls=%fused_computation.16 | loop fusion | flops 1966080 | bytes 1332224 | tf_op jit(solution)/shard_map/convert_element_type | solution.py:19
  91.0 0.7 broadcast_clamp_fusion
  91.7 16.9 %gather_fusion.2 = bf16[4096,256]{1,0:T(8,128)(2,1)} fusion(bf16[4096,256]{1,0:T(8,128)(2,1)S(1)} %copy.91, s32[4096]{0:T(1024)S(1)} %broadcast_clamp_fusion), kind=kCustom, calls=%fused_computation.2 | custom fusion | bytes 4210688 | tf_op jit(solution)/shard_map/jit(_take)/gather | solution.py:217
  108.7 9.7 %gather_fusion.3 = bf16[2816,256]{1,0:T(8,128)(2,1)} fusion(bf16[4096,256]{1,0:T(8,128)(2,1)} %bitcast.24, s32[3072]{0:T(1024)} %pad_clamp_fusion.1), kind=kCustom, calls=%fused_computation.3 | custom fusion | bytes 2894848 | tf_op jit(solution)/shard_map/jit(_take)/gather | solution.py:268
  119.2 4.0 %select_reduce_fusion = s32[2688]{0:T(1024)S(1)} fusion(s32[2048]{0:T(1024)S(1)} %bitcast.167, s32[2688]{0:T(1024)S(1)} %pad_add_fusion.1, s32[2048]{0:T(1024)S(1)} %bitcast.168), kind=kLoop, calls=%fused_computation.11 | loop fusion | flops 16512384 | bytes 37888 | tf_op jit(solution)/shard_map/reduce_max | solution.py:254
  123.3 1.1 gather_fusion.6
  124.8 1.4 gather_fusion.7
  126.2 1.4 gather_fusion.4
  128.2 1.2 fusion.166
  129.5 1.6 cosine_convert_fusion.1
  131.0 1.1 all-gather.5.cloned.1.call-done.near
  132.1 1.0 fusion.193
  133.2 0.8 fusion.25
  134.0 1.3 fusion.188
  135.3 1.0 fusion.57
  136.3 1.1 fusion.46.query
  137.4 3.7 %collective-permute-start = (bf16[128,256]{1,0:T(8,128)(2,1)S(1)}, bf16[128,256]{1,0:T(8,128)(2,1)S(1)}, u32[]{:S(2)}, u32[]{:S(2)}) collective-permute-start(bf16[128,256]{1,0:T(8,128)(2,1)S(1)} %fusion.57), channel_id=1, source_target_pairs={{0,16},{2,18},{4,20},{6,22},{8,24},{10,26},{12,28},{14,30},{16,0},... | collective-permute-start | bytes 196616 | tf_op jit(solution)/shard_map/ppermute | solution.py:109
  141.1 2.7 collective-permute-done
  143.9 2.0 collective-permute-start.1
  145.8 3.1 %collective-permute-done.1 = bf16[256,256]{1,0:T(8,128)(2,1)S(1)} collective-permute-done((bf16[256,256]{1,0:T(8,128)(2,1)S(1)}, bf16[256,256]{1,0:T(8,128)(2,1)S(1)}, u32[]{:S(2)}, u32[]{:S(2)}) %collective-permute-start.1) | collective-permute-done | bytes 131104 | tf_op jit(solution)/shard_map/ppermute | solution.py:109
  148.9 2.3 collective-permute-start.2
  151.2 4.4 %collective-permute-done.2 = bf16[512,256]{1,0:T(8,128)(2,1)S(1)} collective-permute-done((bf16[512,256]{1,0:T(8,128)(2,1)S(1)}, bf16[512,256]{1,0:T(8,128)(2,1)S(1)}, u32[]{:S(2)}, u32[]{:S(2)}) %collective-permute-start.2) | collective-permute-done | bytes 262176 | tf_op jit(solution)/shard_map/ppermute | solution.py:109
  155.5 1.4 collective-permute-start.3
  158.8 0.7 constant_dynamic-update-slice_fusion.1
  159.6 6.3 %collective-permute-done.3 = bf16[1024,256]{1,0:T(8,128)(2,1)S(1)} collective-permute-done((bf16[1024,256]{1,0:T(8,128)(2,1)S(1)}, bf16[1024,256]{1,0:T(8,128)(2,1)S(1)}, u32[]{:S(2)}, u32[]{:S(2)}) %collective-permute-start.3) | collective-permute-done | bytes 524320 | tf_op jit(solution)/shard_map/ppermute | solution.py:109
  165.9 0.9 constant_dynamic-update-slice_fusion
  166.8 10.4 %all-to-all-start.3 = ((bf16[16,256,256]{2,1,0:T(8,128)(2,1)}), bf16[16,256,256]{2,1,0:T(8,128)(2,1)}, u32[]{:S(2)}, u32[]{:S(2)}) async-start(bf16[16,256,256]{2,1,0:T(8,128)(2,1)} %bitcast.131), calls=%async_computation.3 | async-start | bytes 4194304 | tf_op jit(solution)/shard_map/all_to_all | solution.py:102
  177.5 1.5 reduce_max.12
  179.0 2.1 and_compare_fusion
  181.9 1.4 slice_bitcast_fusion
  183.3 1.8 copy-done.1
  185.1 3.4 %shard_map.212 = f32[128,256]{1,0:T(8,128)S(1)} custom-call(bf16[2816,512]{1,0:T(8,128)(2,1)S(1)} %copy-done.1, bf16[2560,128]{1,0:T(8,128)(2,1)S(1)} %get-tuple-element.57.code, f32[128,256]{1,0:T(8,128)S(1)} %fusion.46.query, bf16[512,512]{1,0:T(8,128)(2,1)S(1)} %pad_maximum_fusion.2.wide, bf16[128,512]{1,0:T(8,128)(2,1)S(1)} %pad_maximum_fusion.5.twide), custom_call_target="tpu_custom_call" | custom-call | flops 1677721600 | bytes 3801088 | tf_op jit(solution)/shard_map/pallas_call | solution.py:79
  188.4 2.2 all_gather.13
  190.7 1.1 fusion.7
  192.5 25.7 %all-to-all-done.3 = bf16[16,256,256]{2,1,0:T(8,128)(2,1)} async-done(((bf16[16,256,256]{2,1,0:T(8,128)(2,1)}), bf16[16,256,256]{2,1,0:T(8,128)(2,1)}, u32[]{:S(2)}, u32[]{:S(2)}) %all-to-all-start.3) | async-done | bytes 2097184 | tf_op jit(solution)/shard_map/all_to_all | solution.py:102
  218.1 3.8 %pad_maximum_fusion = bf16[6144,256]{1,0:T(8,128)(2,1)} fusion(bf16[2048,256]{1,0:T(8,128)(2,1)} %constant_dynamic-update-slice_fusion, bf16[4096,256]{1,0:T(8,128)(2,1)} %bitcast.39), kind=kLoop, calls=%fused_computation.15 | loop fusion | flops 6291456 | bytes 6291456 | tf_op jit(solution)/shard_map/concatenate | solution.py:260
  221.9 9.7 %gather_fusion.5 = bf16[2816,256]{1,0:T(8,128)(2,1)} fusion(bf16[6144,256]{1,0:T(8,128)(2,1)} %pad_maximum_fusion, s32[3072]{0:T(1024)S(1)} %pad_clamp_fusion), kind=kCustom, calls=%fused_computation.6 | custom fusion | bytes 2894848 | tf_op jit(solution)/shard_map/jit(_take)/gather | solution.py:268
  233.0 6.9 %scatter_custom_fusion = bf16[4096,256]{1,0:T(8,128)(2,1)} fusion(bf16[4096,256]{1,0:T(8,128)(2,1)} %copy-done.3, s32[256]{0:T(256)S(1)} %bitcast.171, bf16[2048,256]{1,0:T(8,128)(2,1)} %constant_dynamic-update-slice_fusion, s32[1024]{0:T(1024)S(1)} %pad_clamp_fusion.4), kind=kCustom, calls=%fused_computation.157 | custom fusion | bytes 2097152 | tf_op jit(solution)/shard_map/scatter | solution.py:126
  239.8 7.4 %all-gather.7.cloned.1.call-done.near = bf16[2816,512]{1,0:T(8,128)(2,1)} async-done(((bf16[2816,256]{1,0:T(8,128)(2,1)}), bf16[2816,512]{1,0:T(8,128)(2,1)}) %all-gather.7.cloned.1.call-update) | async-done | bytes 2883600 | tf_op jit(solution)/shard_map/all_gather | solution.py:271
  247.2 1.1 fusion.192
  248.4 2.3 fusion.33
  251.2 1.0 fusion.59
  252.4 3.4 %shard_map.213 = f32[128,256]{1,0:T(8,128)S(1)} custom-call(bf16[2816,512]{1,0:T(8,128)(2,1)S(1)} %copy-done.2, bf16[2560,128]{1,0:T(8,128)(2,1)S(1)} %get-tuple-element.56.code, f32[128,256]{1,0:T(8,128)S(1)} %fusion.44.query, bf16[512,512]{1,0:T(8,128)(2,1)S(1)} %pad_maximum_fusion.2.wide, bf16[128,512]{1,0:T(8,128)(2,1)S(1)} %pad_maximum_fusion.5.twide), custom_call_target="tpu_custom_call" | custom-call | flops 1677721600 | bytes 3801088 | tf_op jit(solution)/shard_map/pallas_call | solution.py:79
  255.8 2.0 all_gather.15
  257.8 0.8 convolution_convert_fusion
  258.6 6.8 %all-to-all-start.4 = ((bf16[16,16,256]{2,1,0:T(8,128)(2,1)}), bf16[16,16,256]{2,1,0:T(8,128)(2,1)S(1)}, u32[]{:S(2)}, u32[]{:S(2)}) async-start(bf16[16,16,256]{2,1,0:T(8,128)(2,1)} %bitcast.49), calls=%async_computation.4 | async-start | bytes 262144 | tf_op jit(solution)/shard_map/all_to_all | solution.py:102
  265.4 1.1 fusion.8
  266.6 0.8 pad_maximum_fusion.6
  267.5 5.8 %all-to-all-done.4 = bf16[16,16,256]{2,1,0:T(8,128)(2,1)S(1)} async-done(((bf16[16,16,256]{2,1,0:T(8,128)(2,1)}), bf16[16,16,256]{2,1,0:T(8,128)(2,1)S(1)}, u32[]{:S(2)}, u32[]{:S(2)}) %all-to-all-start.4) | async-done | bytes 131104 | tf_op jit(solution)/shard_map/all_to_all | solution.py:102
  273.3 4.8 %scatter_fusion = bf16[4096,256]{1,0:T(8,128)(2,1)} fusion(bf16[4096,256]{1,0:T(8,128)(2,1)} %scatter_custom_fusion, s32[256]{0:T(256)S(1)} %bitcast.169, bf16[256,256]{1,0:T(8,128)(2,1)S(1)} %bitcast.137), kind=kCustom, calls=%fused_computation.10 | custom fusion | bytes 394240 | tf_op jit(solution)/shard_map/scatter | solution.py:126
  (230 shorter events, 21.0 us)
Async XLA Ops:
  7.2 129.1 %copy-start = (bf16[512,512]{1,0:T(8,128)(2,1)S(1)}, bf16[512,512]{1,0:T(8,128)(2,1)}, u32[]{:S(2)}) copy-start(bf16[512,512]{1,0:T(8,128)(2,1)} %param.36) | copy-start | bytes 1572868
  7.2 1.8 copy-start.40
  7.2 2.1 copy-start.41
  7.2 2.4 copy-start.44
  7.2 3.8 %copy-start.14 = (s32[2,64,40,1]{1,3,2,0:T(1,128)S(1)}, s32[2,64,40,1]{1,3,2,0:T(1,128)}, u32[]{:S(2)}) copy-start(s32[2,64,40,1]{1,3,2,0:T(1,128)} %param.28) | copy-start | bytes 61444
  7.2 4.9 %copy-start.15 = (s32[2,64,40]{1,2,0:T(8,128)S(1)}, s32[2,64,40]{1,2,0:T(8,128)}, u32[]{:S(2)}) copy-start(s32[2,64,40]{1,2,0:T(8,128)} %param.29) | copy-start | bytes 61444
  8.9 82.8 %copy-start.3 = (bf16[4096,256]{1,0:T(8,128)(2,1)}, bf16[4096,256]{1,0:T(8,128)(2,1)S(1)}, u32[]{:S(2)}) copy-start(bf16[4096,256]{1,0:T(8,128)(2,1)S(1)} %copy.91) | copy-start | bytes 6291460
  10.6 62.1 %copy-start.33 = (s32[2,128]{1,0:T(2,128)}, s32[2,128]{1,0:T(2,128)S(1)}, u32[]{:S(2)}) copy-start(s32[2,128]{1,0:T(2,128)S(1)} %get-tuple-element.102) | copy-start | bytes 3076
  12.3 3.9 %copy-start.37 = (s32[2,64]{1,0:T(2,128)S(1)}, s32[2,64]{1,0:T(2,128)}, u32[]{:S(2)}) copy-start(s32[2,64]{1,0:T(2,128)} %param.26) | copy-start | bytes 1540
  12.4 1.1 copy-start.11
  13.5 1.8 copy-start.13
  13.5 19.7 %copy-start.4 = (s32[4096]{0:T(1024)S(1)}, s32[4096]{0:T(1024)}, u32[]{:S(2)}) copy-start(s32[4096]{0:T(1024)} %param.22) | copy-start | bytes 49156
  16.5 15.9 %copy-start.39 = (s32[128]{0:T(128)}, s32[128]{0:T(128)S(1)}, u32[]{:S(2)}) copy-start(s32[128]{0:T(128)S(1)} %broadcast_in_dim.256) | copy-start | bytes 1540
  37.1 20.5 %all-to-all-start.1 = ((s32[16,1,32]{2,1,0:T(1,128)}), s32[16,1,32]{2,1,0:T(1,128)S(1)}, u32[]{:S(2)}, u32[]{:S(2)}) async-start(s32[16,1,32]{2,1,0:T(1,128)} %all_to_all.28), calls=%async_computation.1 | async-start | bytes 16384 | tf_op jit(solution)/shard_map/all_to_all | solution.py:102
  57.6 0.6 copy-start.17
  58.1 50.5 %all-to-all-start.2 = ((bf16[16,256,256]{2,1,0:T(8,128)(2,1)}), bf16[16,256,256]{2,1,0:T(8,128)(2,1)}, u32[]{:S(2)}, u32[]{:S(2)}) async-start(bf16[16,256,256]{2,1,0:T(8,128)(2,1)} %bitcast.132), calls=%async_computation.2 | async-start | bytes 4194304 | tf_op jit(solution)/shard_map/all_to_all | solution.py:102
  65.1 5.0 %copy-start.16 = (s32[2,64,40]{1,2,0:T(8,128)S(1)}, s32[2,64,40]{1,2,0:T(8,128)}, u32[]{:S(2)}) copy-start(s32[2,64,40]{1,2,0:T(8,128)} %param.30) | copy-start | bytes 61444
  65.1 67.1 %all-gather.5.cloned.1.call-start = ((), (), s32[]{:S(2)}) async-start(), calls=%async_computation.5 | async-start | bytes 4325376 | tf_op jit(solution)/shard_map/all_gather | solution.py:271
  76.9 2.1 copy-start.35
  108.7 10.3 %copy-start.42 = (s32[128]{0:T(128)S(1)}, s32[128]{0:T(128)}, u32[]{:S(2)}) copy-start(s32[128]{0:T(128)} %get-tuple-element.89) | copy-start | bytes 1540
  108.7 10.3 %copy-start.34 = (f32[2,3,256]{2,0,1:T(2,128)S(1)}, f32[2,3,256]{2,0,1:T(2,128)}, u32[]{:S(2)}) copy-start(f32[2,3,256]{2,0,1:T(2,128)} %param.35) | copy-start | bytes 18436
  108.7 10.4 %copy-start.19 = (bf16[2,64,128]{2,1,0:T(8,128)(2,1)S(1)}, bf16[2,64,128]{2,1,0:T(8,128)(2,1)}, u32[]{:S(2)}) copy-start(bf16[2,64,128]{2,1,0:T(8,128)(2,1)} %param.27) | copy-start | bytes 98308
  118.4 6.1 %copy-start.18 = (s32[16,1,32]{2,1,0:T(1,128)S(1)}, s32[16,1,32]{2,1,0:T(1,128)}, u32[]{:S(2)}) copy-start(s32[16,1,32]{2,1,0:T(1,128)} %copy-done.17) | copy-start | bytes 6148
  118.4 14.8 %copy-start.5 = (bf16[1280,3,256]{0,2,1:T(8,128)(2,1)S(1)}, bf16[1280,3,256]{0,2,1:T(8,128)(2,1)}, u32[]{:S(2)}) copy-start(bf16[1280,3,256]{0,2,1:T(8,128)(2,1)} %copy.65) | copy-start | bytes 5898244
  119.1 16.2 %copy-start.23 = (f32[1,1,256]{2,0,1:T(1,128)}, f32[1,1,256]{2,0,1:T(1,128)S(1)}, u32[]{:S(2)}) copy-start(f32[1,1,256]{2,0,1:T(1,128)S(1)} %get-tuple-element.74) | copy-start | bytes 3076
  119.1 16.2 %copy-start.25 = (f32[1,1,256]{2,0,1:T(1,128)}, f32[1,1,256]{2,0,1:T(1,128)S(1)}, u32[]{:S(2)}) copy-start(f32[1,1,256]{2,0,1:T(1,128)S(1)} %get-tuple-element.75) | copy-start | bytes 3076
  119.1 16.2 %copy-start.27 = (f32[1,1,256]{2,0,1:T(1,128)}, f32[1,1,256]{2,0,1:T(1,128)S(1)}, u32[]{:S(2)}) copy-start(f32[1,1,256]{2,0,1:T(1,128)S(1)} %get-tuple-element.76) | copy-start | bytes 3076
  119.1 16.2 %copy-start.29 = (f32[1,1,256]{2,0,1:T(1,128)}, f32[1,1,256]{2,0,1:T(1,128)S(1)}, u32[]{:S(2)}) copy-start(f32[1,1,256]{2,0,1:T(1,128)S(1)} %get-tuple-element.77) | copy-start | bytes 3076
  119.1 16.2 %copy-start.31 = (f32[1,1,256]{2,0,1:T(1,128)}, f32[1,1,256]{2,0,1:T(1,128)S(1)}, u32[]{:S(2)}) copy-start(f32[1,1,256]{2,0,1:T(1,128)S(1)} %get-tuple-element.78) | copy-start | bytes 3076
  137.4 6.4 %collective-permute-start = (bf16[128,256]{1,0:T(8,128)(2,1)S(1)}, bf16[128,256]{1,0:T(8,128)(2,1)S(1)}, u32[]{:S(2)}, u32[]{:S(2)}) collective-permute-start(bf16[128,256]{1,0:T(8,128)(2,1)S(1)} %fusion.57), channel_id=1, source_target_pairs={{0,16},{2,18},{4,20},{6,22},{8,24},{10,26},{12,28},{14,30},{16,0},... | collective-permute-start | bytes 196616 | tf_op jit(solution)/shard_map/ppermute | solution.py:109
  143.9 5.0 %collective-permute-start.1 = (bf16[256,256]{1,0:T(8,128)(2,1)S(1)}, bf16[256,256]{1,0:T(8,128)(2,1)S(1)}, u32[]{:S(2)}, u32[]{:S(2)}) collective-permute-start(bf16[256,256]{1,0:T(8,128)(2,1)S(1)} %pad_maximum_fusion.4), channel_id=1, source_target_pairs={{0,8},{2,10},{4,12},{6,14},{8,0},{10,2},{12,4},{14,6},{16,24},{18,... | collective-permute-start | bytes 393224 | tf_op jit(solution)/shard_map/ppermute | solution.py:109
  148.9 6.6 %collective-permute-start.2 = (bf16[512,256]{1,0:T(8,128)(2,1)S(1)}, bf16[512,256]{1,0:T(8,128)(2,1)S(1)}, u32[]{:S(2)}, u32[]{:S(2)}) collective-permute-start(bf16[512,256]{1,0:T(8,128)(2,1)S(1)} %pad_maximum_fusion.3), channel_id=1, source_target_pairs={{0,4},{2,6},{4,0},{6,2},{8,12},{10,14},{12,8},{14,10},{16,20},{18,... | collective-permute-start | bytes 786440 | tf_op jit(solution)/shard_map/ppermute | solution.py:109
  155.5 10.3 %collective-permute-start.3 = (bf16[1024,256]{1,0:T(8,128)(2,1)S(1)}, bf16[1024,256]{1,0:T(8,128)(2,1)S(1)}, u32[]{:S(2)}, u32[]{:S(2)}) collective-permute-start(bf16[1024,256]{1,0:T(8,128)(2,1)S(1)} %pad_maximum_fusion.1), channel_id=1, source_target_pairs={{0,2},{2,0},{4,6},{6,4},{8,10},{10,8},{12,14},{14,12},{16,18},{18,... | collective-permute-start | bytes 1572872 | tf_op jit(solution)/shard_map/ppermute | solution.py:109
  166.8 10.5 %copy-start.38 = (s32[128]{0:T(128)S(1)}, s32[128]{0:T(128)}, u32[]{:S(2)}) copy-start(s32[128]{0:T(128)} %get-tuple-element.41) | copy-start | bytes 1540
  166.8 10.6 %copy-start.21 = (bf16[128,512]{1,0:T(8,128)(2,1)S(1)}, bf16[128,512]{1,0:T(8,128)(2,1)}, u32[]{:S(2)}) copy-start(bf16[128,512]{1,0:T(8,128)(2,1)} %param.40) | copy-start | bytes 393220
  166.8 10.6 %copy-start.22 = (bf16[128,512]{1,0:T(8,128)(2,1)S(1)}, bf16[128,512]{1,0:T(8,128)(2,1)}, u32[]{:S(2)}) copy-start(bf16[128,512]{1,0:T(8,128)(2,1)} %param.39) | copy-start | bytes 393220
  166.8 10.7 %copy-start.9 = (bf16[512,512]{1,0:T(8,128)(2,1)S(1)}, bf16[512,512]{1,0:T(8,128)(2,1)}, u32[]{:S(2)}) copy-start(bf16[512,512]{1,0:T(8,128)(2,1)} %param.38) | copy-start | bytes 1572868
  166.8 10.7 %copy-start.10 = (bf16[512,512]{1,0:T(8,128)(2,1)S(1)}, bf16[512,512]{1,0:T(8,128)(2,1)}, u32[]{:S(2)}) copy-start(bf16[512,512]{1,0:T(8,128)(2,1)} %param.37) | copy-start | bytes 1572868
  166.8 51.4 %all-to-all-start.3 = ((bf16[16,256,256]{2,1,0:T(8,128)(2,1)}), bf16[16,256,256]{2,1,0:T(8,128)(2,1)}, u32[]{:S(2)}, u32[]{:S(2)}) async-start(bf16[16,256,256]{2,1,0:T(8,128)(2,1)} %bitcast.131), calls=%async_computation.3 | async-start | bytes 4194304 | tf_op jit(solution)/shard_map/all_to_all | solution.py:102
  177.2 70.0 %all-gather.7.cloned.1.call-start = ((), (), s32[]{:S(2)}) async-start(), calls=%async_computation.6 | async-start | bytes 4325376 | tf_op jit(solution)/shard_map/all_gather | solution.py:271
  181.1 0.7 copy-start.12
  181.1 0.7 copy-start.43
  183.3 1.8 copy-start.1
  185.1 5.6 %copy-start.6 = (bf16[512,512]{1,0:T(8,128)(2,1)S(1)}, bf16[512,512]{1,0:T(8,128)(2,1)}, u32[]{:S(2)}) copy-start(bf16[512,512]{1,0:T(8,128)(2,1)} %param.41) | copy-start | bytes 1572868
  231.6 16.8 %copy-start.20 = (bf16[128,128]{1,0:T(8,128)(2,1)S(1)}, bf16[128,128]{1,0:T(8,128)(2,1)}, u32[]{:S(2)}) copy-start(bf16[128,128]{1,0:T(8,128)(2,1)} %get-tuple-element.83) | copy-start | bytes 98308
  247.2 3.6 %copy-start.2 = (bf16[2816,512]{1,0:T(8,128)(2,1)S(1)}, bf16[2816,512]{1,0:T(8,128)(2,1)}, u32[]{:S(2)}) copy-start(bf16[2816,512]{1,0:T(8,128)(2,1)} %all-gather.7.cloned.1.call-done.near) | copy-start | bytes 8650756
  248.4 2.8 copy-start.24
  248.4 2.8 copy-start.26
  248.4 2.8 copy-start.28
  248.4 2.8 copy-start.30
  248.4 2.8 copy-start.32
  252.4 5.4 %copy-start.36 = (s32[128]{0:T(128)S(1)}, s32[128]{0:T(128)}, u32[]{:S(2)}) copy-start(s32[128]{0:T(128)} %copy-done.35) | copy-start | bytes 1540
  252.4 13.1 %copy-start.7 = (bf16[512,512]{1,0:T(8,128)(2,1)S(1)}, bf16[512,512]{1,0:T(8,128)(2,1)}, u32[]{:S(2)}) copy-start(bf16[512,512]{1,0:T(8,128)(2,1)} %param.41) | copy-start | bytes 1572868
  252.4 14.2 %copy-start.8 = (bf16[64,2,256]{2,1,0:T(2,128)(2,1)S(1)}, bf16[64,2,256]{2,1,0:T(2,128)(2,1)}, u32[]{:S(2)}) copy-start(bf16[64,2,256]{2,1,0:T(2,128)(2,1)} %reshape.580) | copy-start | bytes 196612
  258.6 14.7 %all-to-all-start.4 = ((bf16[16,16,256]{2,1,0:T(8,128)(2,1)}), bf16[16,16,256]{2,1,0:T(8,128)(2,1)S(1)}, u32[]{:S(2)}, u32[]{:S(2)}) async-start(bf16[16,16,256]{2,1,0:T(8,128)(2,1)} %bitcast.49), calls=%async_computation.4 | async-start | bytes 262144 | tf_op jit(solution)/shard_map/all_to_all | solution.py:102
Sparse Core Ops, SparseCore 0:
  118.5 13.5 all-gather.4
  231.7 15.4 all-gather.6
